TPU v7x, 32 devices: a whole 2x2x4 slice. The times are simulated.
32 devices in a mesh: exp: 4 (over z), row: 4 (over y, x), col: 2 (over core).
Axes of the slice: x: 2, y: 2, z: 4, core: 2. Of those that a mesh axis runs over, the one named last changes fastest.
Arguments:
- tokens: bfloat16 [4096, 768], P(('exp', 'col')), may hold values from -6 to 6
- qkv_weight: bfloat16 [3, 768, 768], P(None, ('exp', 'col'), 'row'), may hold values from -0.21875 to 0.21875
- out_weight: bfloat16 [768, 768], P('row', ('exp', 'col')), may hold values from -1.25 to 1.25
- bias_table: bfloat16 [32, 12], P(None, 'row'), may hold values from -4 to 4
- gain_attn: bfloat16 [768], P(('exp', 'col')), may hold values from 0.5 to 1.5
- gain_expert: bfloat16 [768], P(('exp', 'col')), may hold values from 0.5 to 1.5
- router_weight: bfloat16 [768, 8], P(('exp', 'col')), may hold values from -0.15625 to 0.15625
- expert_in: bfloat16 [8, 768, 3072], P(('exp', 'col'), None, 'row'), may hold values from -0.21875 to 0.21875
- expert_out: bfloat16 [8, 3072, 768], P(('exp', 'col'), 'row'), may hold values from -6 to 6
- lengths: int32 [8], P(('exp', 'col')), may hold values from 1 to 512, 3072 in all
- routes: int32 [4096, 1], P(('exp', 'col')), may hold values from 0 to 7
- cotangent: bfloat16 [4096, 768], P(('exp', 'col')), may hold values from -6 to 6
Outputs:
- result: bfloat16 [4096, 768], P(('exp', 'col'))
- grad_tokens: bfloat16 [4096, 768], P(('exp', 'col'))
- grad_qkv_weight: float32 [3, 768, 768], P(None, ('exp', 'col'), 'row')
- grad_out_weight: float32 [768, 768], P('row', ('exp', 'col'))
- grad_bias_table: float32 [32, 12], P(None, 'row')
- grad_gain_attn: float32 [768], P(('exp', 'col'))
- grad_gain_expert: float32 [768], P(('exp', 'col'))
- grad_router: float32 [768, 8], P(('exp', 'col'))
- grad_expert_in: float32 [8, 768, 3072], P(('exp', 'col'), None, 'row')
- grad_expert_out: float32 [8, 3072, 768], P(('exp', 'col'), 'row')
All inputs are finite; a program needn't handle non-finite values. No bound on the sum of `lengths` on one device may be relied on, other than what follows from the above.
Results may differ from a plain program's by a relative error of at most 0.015.
Values may be sent and summed in bfloat16 or wider, within the bound.
A program may use at most 128 MiB of HBM per device.

v0:
```python
import jax
import jax.numpy as jnp
import numpy as np
from jax import lax
from jax.sharding import PartitionSpec as P

DH = 64
CAP = 8


epsilon = 1e-06
thresholds = np.array([12, 16, 23, 32, 46, 64, 91], dtype=np.int32)
highest = lax.Precision.HIGHEST


def bucket_of(offset):
    distance = jnp.abs(offset)
    beyond = jnp.sum((distance[..., None] >= jnp.asarray(thresholds)).astype(jnp.int32), axis=-1)
    return (offset > 0).astype(jnp.int32) * 16 + jnp.minimum(distance, 8) + beyond


def normalize(values, gain_row):
    inv_root = lax.rsqrt(jnp.mean(values * values, axis=-1, keepdims=True) + epsilon)
    unit_rows = values * inv_root
    return (unit_rows * gain_row, unit_rows, inv_root)


def normalize_back(grad_in, unit_rows, inv_root, gain_row):
    scaled = grad_in * gain_row
    grad_rows = inv_root * (
        scaled - unit_rows * jnp.mean(scaled * unit_rows, axis=-1, keepdims=True)
    )
    return (grad_rows, jnp.sum(grad_in * unit_rows, axis=0))


def toeplitz(rel_rows, length):
    head_count = rel_rows.shape[0]
    flattened = jnp.tile(rel_rows, (1, length))[:, : length * (2 * length - 1)]
    return flattened.reshape(head_count, length, 2 * length - 1)[:, :, length - 1 :]


def diagonal_sums(score_grid, length):
    head_count = score_grid.shape[0]
    padded = jnp.pad(score_grid, ((0, 0), (0, 0), (length - 1, 0)))
    flattened = jnp.pad(
        padded.reshape(head_count, length * (2 * length - 1)), ((0, 0), (0, length))
    )
    return jnp.sum(flattened.reshape(head_count, length, 2 * length), axis=1)


def expert_forward(arrived, expert_in, expert_out):
    before_act = jnp.einsum(
        "necd,edf->necf", arrived, expert_in, preferred_element_type=jnp.float32
    )
    acted = jax.nn.gelu(before_act).astype(jnp.bfloat16)
    partial_out = jnp.einsum(
        "necf,efd->necd", acted, expert_out, preferred_element_type=jnp.float32
    )
    return (before_act, acted, partial_out)


def expert_backward(arrived, before_act, acted, grad_arrived, expert_in, expert_out):
    grad_expert_out = jnp.einsum(
        "necf,necd->efd", acted, grad_arrived, preferred_element_type=jnp.float32
    )
    grad_acted = jnp.einsum(
        "necd,efd->necf", grad_arrived, expert_out, preferred_element_type=jnp.float32
    )
    gelu_value, gelu_back = jax.vjp(jax.nn.gelu, before_act)
    grad_before = gelu_back(grad_acted)[0].astype(jnp.bfloat16)
    grad_expert_in = jnp.einsum(
        "necd,necf->edf", arrived, grad_before, preferred_element_type=jnp.float32
    )
    grad_arrived_in = jnp.einsum(
        "necf,edf->necd", grad_before, expert_in, preferred_element_type=jnp.float32
    )
    return (grad_expert_in, grad_expert_out, grad_arrived_in)


def body(
    tokens,
    qkv_weight,
    out_weight,
    bias_table,
    gain_attn,
    gain_expert,
    router_weight,
    expert_in,
    expert_out,
    lengths,
    routes,
    cotangent,
):
    full_qkv, full_out, full_router, gain_one, gain_two = (
        lax.all_gather(qkv_weight, ("exp", "col"), axis=1, tiled=True),
        lax.all_gather(out_weight, ("exp", "col"), axis=1, tiled=True),
        lax.all_gather(router_weight, ("exp", "col"), axis=0, tiled=True),
        lax.all_gather(gain_attn, ("exp", "col"), axis=0, tiled=True),
        lax.all_gather(gain_expert, ("exp", "col"), axis=0, tiled=True),
    )
    token_count = tokens.shape[0]
    model_width = tokens.shape[1]
    rows_in = tokens.astype(jnp.float32)
    normed_one, unit_one, scale_one = normalize(rows_in, gain_one.astype(jnp.float32))
    hidden_one = normed_one.astype(jnp.bfloat16)
    projected = jnp.einsum(
        "td,sde->ste", hidden_one, full_qkv, preferred_element_type=jnp.float32
    ).astype(jnp.bfloat16)
    windows = lengths.shape[0]
    window_len = token_count // windows
    local_heads = qkv_weight.shape[2] // DH
    factor = DH ** (-0.5)
    shaped = projected.reshape(3, windows, window_len, local_heads, DH)
    query_low = shaped[0]
    key_low = shaped[1]
    value_low = shaped[2]
    offsets = jnp.arange(2 * window_len, dtype=jnp.int32) - (window_len - 1)
    picks = (
        bucket_of(offsets)[:, None] == jnp.arange(bias_table.shape[0], dtype=jnp.int32)[None, :]
    ).astype(jnp.bfloat16)
    rel_bias = jnp.einsum("jb,bh->hj", picks, bias_table, preferred_element_type=jnp.float32)
    bias_grid = toeplitz(rel_bias, window_len)
    key_valid = jnp.arange(window_len, dtype=jnp.int32)[None, :] < lengths[:, None]

    def attention_scores():
        raw_scores = (
            jnp.einsum("wqhd,wkhd->whqk", query_low, key_low, preferred_element_type=jnp.float32)
            * factor
            + bias_grid[None]
        )
        return jnp.where(key_valid[:, None, None, :], raw_scores, -1e30)

    logits_attn = attention_scores()
    row_max = jnp.max(logits_attn, axis=-1, keepdims=True)
    weights_exp = jnp.exp(logits_attn - row_max)
    denominator = jnp.sum(weights_exp, axis=-1, keepdims=True)
    log_total = row_max + jnp.log(denominator)
    probs_low = (weights_exp / denominator).astype(jnp.bfloat16)
    attended = jnp.einsum(
        "whqk,wkhd->wqhd", probs_low, value_low, preferred_element_type=jnp.float32
    )
    heads_low = attended.reshape(token_count, local_heads * DH).astype(jnp.bfloat16)
    attn_out = lax.psum(jnp.dot(heads_low, full_out, preferred_element_type=jnp.float32), "row")
    mixed = rows_in + attn_out
    normed_two, unit_two, scale_two = normalize(mixed, gain_two.astype(jnp.float32))
    hidden_two = normed_two.astype(jnp.bfloat16)
    router_logits = jnp.dot(hidden_two, full_router, preferred_element_type=jnp.float32)
    router_probs = jax.nn.softmax(router_logits, axis=-1)
    experts = full_router.shape[1]
    local_experts = expert_in.shape[0]
    groups = experts // local_experts
    chosen = routes[:, 0]
    route_hot = chosen[:, None] == jnp.arange(experts, dtype=jnp.int32)[None, :]
    gate_prob = jnp.sum(jnp.where(route_hot, router_probs, 0.0), axis=-1)
    position = jnp.arange(token_count, dtype=jnp.int32)
    is_live = position % window_len < jnp.repeat(lengths, window_len)
    live_hot = (route_hot & is_live[:, None]).astype(jnp.int32)
    earlier = jnp.cumsum(live_hot, axis=0) - live_hot
    slot_rank = jnp.sum(jnp.where(route_hot, earlier, 0), axis=-1)
    is_kept = is_live & (slot_rank < CAP)
    target = chosen * CAP + slot_rank
    target_safe = jnp.where(is_kept, target, 0)
    slot_ids = jnp.arange(experts * CAP, dtype=jnp.int32)
    matches = (target[None, :] == slot_ids[:, None]) & is_kept[None, :]
    source_row = jnp.sum(jnp.where(matches, position[None, :], 0), axis=1)
    filled = jnp.any(matches, axis=1)
    outgoing = jnp.where(
        filled[:, None], hidden_two[source_row], jnp.zeros((), jnp.bfloat16)
    ).reshape(experts, CAP, model_width)
    upstream = cotangent.astype(jnp.float32)
    grad_result = (gate_prob[:, None] * upstream).astype(jnp.bfloat16)
    grad_send = jnp.where(
        filled[:, None], grad_result[source_row], jnp.zeros((), jnp.bfloat16)
    ).reshape(experts, CAP, model_width)
    arrived = lax.all_to_all(
        outgoing, ("exp", "col"), split_axis=0, concat_axis=0, tiled=True
    ).reshape(groups, local_experts, CAP, model_width)
    before_act, acted, partial_out = expert_forward(arrived, expert_in, expert_out)
    returned = lax.all_to_all(
        partial_out.reshape(groups * local_experts, CAP, model_width),
        ("exp", "col"),
        split_axis=0,
        concat_axis=0,
        tiled=True,
    )
    per_token = jnp.where(
        is_kept[:, None], returned.reshape(experts * CAP, model_width)[target_safe], 0.0
    )
    expert_result = lax.psum(per_token, "row")
    grad_arrived = lax.all_to_all(
        grad_send, ("exp", "col"), split_axis=0, concat_axis=0, tiled=True
    ).reshape(groups, local_experts, CAP, model_width)
    grad_expert_in, grad_expert_out, grad_arrived_in = expert_backward(
        arrived, before_act, acted, grad_arrived, expert_in, expert_out
    )
    grad_back = lax.all_to_all(
        grad_arrived_in.reshape(groups * local_experts, CAP, model_width),
        ("exp", "col"),
        split_axis=0,
        concat_axis=0,
        tiled=True,
    )
    grad_tokens_part = jnp.where(
        is_kept[:, None], grad_back.reshape(experts * CAP, model_width)[target_safe], 0.0
    )
    grad_expert_rows = lax.psum(grad_tokens_part, "row")
    result = mixed + gate_prob[:, None] * expert_result
    grad_gate = jnp.sum(upstream * expert_result, axis=-1)
    grad_logits = router_probs * (
        jnp.where(route_hot, grad_gate[:, None], 0.0) - (gate_prob * grad_gate)[:, None]
    )
    router_rows = full_router.astype(jnp.float32)
    grad_router = jnp.dot(hidden_two.astype(jnp.float32).T, grad_logits, precision=highest)
    grad_hidden_two = grad_expert_rows + jnp.dot(grad_logits, router_rows.T, precision=highest)
    grad_norm_two, grad_gain_two = normalize_back(
        grad_hidden_two, unit_two, scale_two, gain_two.astype(jnp.float32)
    )
    grad_mixed = upstream + grad_norm_two
    grad_attn_low = grad_mixed.astype(jnp.bfloat16)
    grad_out_weight = jnp.einsum(
        "th,td->hd", heads_low, grad_attn_low, preferred_element_type=jnp.float32
    )
    grad_heads = jnp.einsum(
        "td,hd->th", grad_attn_low, full_out, preferred_element_type=jnp.float32
    ).astype(jnp.bfloat16)
    grad_attended = grad_heads.reshape(windows, window_len, local_heads, DH)
    prob_again = jnp.exp(attention_scores() - log_total)
    grad_probs = jnp.einsum(
        "wqhd,wkhd->whqk", grad_attended, value_low, preferred_element_type=jnp.float32
    )
    row_dot = jnp.sum(prob_again * grad_probs, axis=-1, keepdims=True)
    grad_scores = (prob_again * (grad_probs - row_dot)).astype(jnp.bfloat16)
    grad_value = jnp.einsum(
        "whqk,wqhd->wkhd",
        prob_again.astype(jnp.bfloat16),
        grad_attended,
        preferred_element_type=jnp.float32,
    )
    grad_query = (
        jnp.einsum("whqk,wkhd->wqhd", grad_scores, key_low, preferred_element_type=jnp.float32)
        * factor
    )
    grad_key = (
        jnp.einsum("whqk,wqhd->wkhd", grad_scores, query_low, preferred_element_type=jnp.float32)
        * factor
    )
    grad_projected = (
        jnp.stack([grad_query, grad_key, grad_value])
        .reshape(3, token_count, local_heads * DH)
        .astype(jnp.bfloat16)
    )
    grad_rel = diagonal_sums(jnp.sum(grad_scores.astype(jnp.float32), axis=0), window_len)
    grad_table = jnp.dot(picks.astype(jnp.float32).T, grad_rel.T, precision=highest)
    grad_qkv = jnp.einsum(
        "td,ste->sde", hidden_one, grad_projected, preferred_element_type=jnp.float32
    )
    grad_hidden_one = lax.psum(
        jnp.einsum("ste,sde->td", grad_projected, full_qkv, preferred_element_type=jnp.float32),
        "row",
    )
    grad_norm_one, grad_gain_one = normalize_back(
        grad_hidden_one, unit_one, scale_one, gain_one.astype(jnp.float32)
    )
    grad_tokens = (grad_mixed + grad_norm_one).astype(jnp.bfloat16)
    shard_qkv, shard_out, shard_router, shard_gain_one, shard_gain_two = (
        lax.psum_scatter(grad_qkv, ("exp", "col"), scatter_dimension=1, tiled=True),
        lax.psum_scatter(grad_out_weight, ("exp", "col"), scatter_dimension=1, tiled=True),
        lax.psum_scatter(grad_router, ("exp", "col"), scatter_dimension=0, tiled=True),
        lax.psum_scatter(grad_gain_one, ("exp", "col"), scatter_dimension=0, tiled=True),
        lax.psum_scatter(grad_gain_two, ("exp", "col"), scatter_dimension=0, tiled=True),
    )
    table_grad = lax.psum(grad_table, ("exp", "col"))
    return (
        result.astype(jnp.bfloat16),
        grad_tokens,
        shard_qkv,
        shard_out,
        table_grad,
        shard_gain_one,
        shard_gain_two,
        shard_router,
        grad_expert_in,
        grad_expert_out,
    )


def solution(mesh):
    placed = (
        P(("exp", "col"), None),
        P(None, ("exp", "col"), "row"),
        P("row", ("exp", "col")),
        P(None, "row"),
        P(("exp", "col")),
        P(("exp", "col")),
        P(("exp", "col"), None),
        P(("exp", "col"), None, "row"),
        P(("exp", "col"), "row", None),
        P(("exp", "col")),
        P(("exp", "col"), None),
        P(("exp", "col"), None),
    )
    return jax.shard_map(
        body,
        mesh=mesh,
        in_specs=placed,
        out_specs=(
            P(("exp", "col"), None),
            P(("exp", "col"), None),
            P(None, ("exp", "col"), "row"),
            P("row", ("exp", "col")),
            P(None, "row"),
            P(("exp", "col")),
            P(("exp", "col")),
            P(("exp", "col"), None),
            P(("exp", "col"), None, "row"),
            P(("exp", "col"), "row", None),
        ),
        check_vma=False,
    )
```

profile of v0, /device:TPU:0, one launch (start us, length us, event | category | flops | bytes accessed | tf_op | source)
XLA Modules:
  0.0 508.8 jit_solution(15394075302272367241)
XLA Ops:
  8.4 22.2 %all_gather.16 = bf16[3,768,192]{2,0,1:T(4,128)(2,1)S(1)} all-gather(bf16[3,96,192]{2,0,1:T(4,128)(2,1)S(1)} %copy.60), channel_id=1, replica_groups=mesh['exp'=4,'row'=4,'col'=2] {'exp','col'}, dimensions={1}, use_global_device_ids=true | all-gather | bytes 995328 | tf_op jit(solution)/shard_map/all_gather | solution.py:95
  30.6 2.1 copy.61
  34.5 15.3 %all-reduce.8 = (bf16[768]{0:T(1024)(128)(2,1)S(1)}, bf16[768]{0:T(1024)(128)(2,1)S(1)}) all-reduce(bf16[768]{0:T(1024)(128)(2,1)S(1)} %dynamic-update-slice, bf16[768]{0:T(1024)(128)(2,1)S(1)} %dynamic-update-slice.1), channel_id=1, replica_groups=mesh['exp'=4,'row'=4,'col'=2] {'exp','col'}, use_global_device_ids=true, to_apply=%add.2 | all-reduce | flops 1536 | bytes 6144
  50.0 1.9 fusion.47
  53.8 7.6 %copy.85 = f32[1,3,512,1024]{3,1,2,0:T(4,128)} copy(f32[1,3,512,1024]{3,2,1,0:T(8,128)S(1)} %broadcast_bitcast_fusion) | data formatting | bytes 12582912
  61.4 7.9 %slice.42 = f32[3,523776]{1,0:T(4,128)} slice(f32[3,524288]{1,0:T(4,128)} %bitcast.164), slice={[0:3], [0:523776]} | slice | bytes 12570624 | tf_op jit(solution)/shard_map/slice | solution.py:38
  69.3 13.2 %reshape.370 = f32[3,512,1023]{2,1,0:T(8,128)} reshape(f32[3,523776]{1,0:T(4,128)} %slice.42) | data formatting | bytes 12570624 | tf_op jit(solution)/shard_map/reshape | solution.py:39
  82.5 4.7 slice.43
  87.2 3.5 copy.83
  91.5 14.5 %all_gather.17 = bf16[192,768]{0,1:T(8,128)(2,1)S(1)} all-gather(bf16[192,96]{0,1:T(8,128)(2,1)S(1)} %copy.64), channel_id=1, replica_groups=mesh['exp'=4,'row'=4,'col'=2] {'exp','col'}, dimensions={1}, use_global_device_ids=true | all-gather | bytes 331776 | tf_op jit(solution)/shard_map/all_gather | solution.py:96
  105.9 2.9 fusion.100
  112.8 12.7 %all-gather = bf16[8,96,8]{1,2,0:T(8,128)(2,1)S(1)} all-gather(bf16[1,96,8]{1,2,0:T(8,128)(2,1)S(1)} %bitcast.194), channel_id=1, replica_groups=mesh['exp'=4,'row'=4,'col'=2] {'exp','col'}, dimensions={0}, use_global_device_ids=true | all-gather | bytes 13824 | tf_op jit(solution)/shard_map/all_gather | solution.py:97
  129.5 42.6 %all-reduce.13.cloned.1.call-done = f32[512,768]{1,0:T(8,128)} async-done(((f32[512,768]{1,0:T(8,128)}), f32[512,768]{1,0:T(8,128)}) %all-reduce.13.cloned.1.call-update) | async-done | bytes 1572880 | tf_op jit(solution)/shard_map/psum | solution.py:143
  178.1 2.2 fusion.14
  180.3 2.8 gather_fusion.2
  184.7 10.8 %all_to_all.20 = bf16[8,8,768]{2,1,0:T(8,128)(2,1)} all-to-all(bf16[8,8,768]{2,1,0:T(8,128)(2,1)S(1)} %get-tuple-element.69), channel_id=1, replica_groups=mesh['exp'=4,'row'=4,'col'=2] {'exp','col'}, dimensions={0} | all-to-all | bytes 196608 | tf_op jit(solution)/shard_map/all_to_all | solution.py:175
  195.6 4.0 all-to-all-start.2
  201.5 4.4 all-to-all-done.2
  209.6 3.5 all-to-all-start.3
  213.1 2.4 fusion.22
  215.5 5.9 %all-to-all-done.3 = f32[8,8,768]{2,1,0:T(8,128)S(1)} async-done(((f32[8,8,768]{2,1,0:T(8,128)}), f32[8,8,768]{2,1,0:T(8,128)S(1)}, u32[]{:S(2)}, u32[]{:S(2)}) %all-to-all-start.3) | async-done | bytes 196640 | tf_op jit(solution)/shard_map/all_to_all | solution.py:196
  221.3 3.4 all-to-all-start.1
  224.8 2.6 gather_fusion.3
  227.4 5.6 %all-to-all-done.1 = f32[8,8,768]{2,1,0:T(8,128)S(1)} async-done(((f32[8,8,768]{2,1,0:T(8,128)}), f32[8,8,768]{2,1,0:T(8,128)S(1)}, u32[]{:S(2)}, u32[]{:S(2)}) %all-to-all-start.1) | async-done | bytes 196640 | tf_op jit(solution)/shard_map/all_to_all | solution.py:179
  233.0 2.6 gather_fusion.1
  235.6 3.8 broadcast_select_fusion
  240.7 84.1 %all-reduce.17.cloned.1.call-done = (f32[512,768]{1,0:T(8,128)}, f32[512,768]{1,0:T(8,128)}) async-done(((f32[512,768]{1,0:T(8,128)}, f32[512,768]{1,0:T(8,128)}), (f32[512,768]{1,0:T(8,128)}, f32[512,768]{1,0:T(8,128)})) %all-reduce.17.cloned.1.call-update) | async-done | bytes 3145744 | tf_op jit(solution)/shard_map/psum | solution.py:189
  328.4 3.3 multiply_reduce_fusion.1
  331.7 3.0 convert_add_fusion
  336.4 2.3 multiply_reduce_fusion
  340.1 2.8 multiply_convert_fusion
  345.7 2.0 convolution_bitcast_fusion.3
  348.7 1.9 convolution_bitcast_fusion.1
  350.6 2.9 convolution_bitcast_fusion
  355.2 2.0 convolution_bitcast_fusion.2
  357.3 2.9 copy.76
  360.2 2.9 reshape.438
  363.1 2.5 pad.10.clone
  365.6 7.4 %reshape.450 = bf16[1571328]{0:T(1024)(128)(2,1)} reshape(bf16[3,512,1023]{2,1,0:T(8,128)(2,1)S(1)} %pad.10.clone) | data formatting | bytes 6285312
  373.0 5.6 %reshape.381 = bf16[3,523776]{1,0:T(4,128)(2,1)} reshape(bf16[1571328]{0:T(1024)(128)(2,1)} %reshape.450) | data formatting | bytes 6285312 | tf_op jit(solution)/shard_map/reshape | solution.py:46
  378.6 4.2 pad_convert_fusion
  382.9 3.3 bitcast_reduce_fusion
  388.1 11.5 %reduce-scatter.12.cloned.1.call-done = f32[96,192]{1,0:T(8,128)} async-done(((f32[768,192]{1,0:T(8,128)}), f32[96,192]{1,0:T(8,128)}) %reduce-scatter.12.cloned.1.call-update) | async-done | bytes 73744
  401.2 60.6 %all-reduce.15.cloned.1.call-done = f32[512,768]{1,0:T(8,128)} async-done(((f32[512,768]{1,0:T(8,128)}), f32[512,768]{1,0:T(8,128)}) %all-reduce.15.cloned.1.call-update) | async-done | bytes 1572880 | tf_op jit(solution)/shard_map/psum | solution.py:257
  461.9 1.9 fusion.12
  463.8 28.8 %all-reduce.6 = (f32[32,3]{0,1:T(4,128)}, f32[768]{0:T(1024)S(1)}, f32[768]{0:T(1024)S(1)}) all-reduce(f32[32,3]{0,1:T(4,128)S(1)} %fusion.41, f32[768]{0:T(1024)S(1)} %get-tuple-element.52, f32[768]{0:T(1024)S(1)} %copy-done.64), channel_id=1, replica_groups=mesh['exp'=4,'row'=4,'col'=2] {'exp','col'}, use_global_device_ids=true, to_apply=%region_24.25 | all-reduce | flops 1632 | bytes 13056 | tf_op jit(solution)/shard_map/psum | solution.py:272
  493.8 2.8 fusion.11
  496.7 2.9 reduce-scatter.10.cloned.1.call-done
  (233 shorter events, 44.5 us)
Async XLA Ops:
  7.2 192.4 %copy-start = (bf16[1,768,768]{2,1,0:T(8,128)(2,1)S(1)}, bf16[1,768,768]{2,1,0:T(8,128)(2,1)}, u32[]{:S(2)}) copy-start(bf16[1,768,768]{2,1,0:T(8,128)(2,1)} %param.20) | copy-start | bytes 3538948
  7.2 164.9 %all-reduce.13.cloned.1.call-start = ((), (), s32[]{:S(2)}) async-start(), calls=%async_computation.7 | async-start | bytes 3145728 | tf_op jit(solution)/shard_map/psum | solution.py:143
  30.6 3.4 copy-start.73
  30.6 3.6 copy-start.74
  30.6 19.1 %copy-start.10 = (bf16[512,768]{1,0:T(8,128)(2,1)S(1)}, bf16[512,768]{1,0:T(8,128)(2,1)}, u32[]{:S(2)}) copy-start(bf16[512,768]{1,0:T(8,128)(2,1)} %param.13) | copy-start | bytes 2359300
  52.6 53.4 %copy-start.18 = (bf16[1,512,192]{1,2,0:T(8,128)(2,1)}, bf16[1,512,192]{1,2,0:T(8,128)(2,1)S(1)}, u32[]{:S(2)}) copy-start(bf16[1,512,192]{1,2,0:T(8,128)(2,1)S(1)} %get-tuple-element.65) | copy-start | bytes 589828
  52.6 53.4 %copy-start.20 = (bf16[1,512,192]{1,2,0:T(8,128)(2,1)}, bf16[1,512,192]{1,2,0:T(8,128)(2,1)S(1)}, u32[]{:S(2)}) copy-start(bf16[1,512,192]{1,2,0:T(8,128)(2,1)S(1)} %get-tuple-element.66) | copy-start | bytes 589828
  52.6 56.7 %copy-start.23 = (bf16[1,512,192]{1,2,0:T(8,128)(2,1)}, bf16[1,512,192]{1,2,0:T(8,128)(2,1)S(1)}, u32[]{:S(2)}) copy-start(bf16[1,512,192]{1,2,0:T(8,128)(2,1)S(1)} %get-tuple-element.67) | copy-start | bytes 589828
  87.2 4.2 copy-start.48
  105.9 5.2 %copy-start.16 = (bf16[192,768]{0,1:T(8,128)(2,1)}, bf16[192,768]{0,1:T(8,128)(2,1)S(1)}, u32[]{:S(2)}) copy-start(bf16[192,768]{0,1:T(8,128)(2,1)S(1)} %all_gather.17) | copy-start | bytes 884740
  111.2 15.1 %copy-start.36 = (s32[512,1]{0,1:T(1,128)S(1)}, s32[512,1]{0,1:T(1,128)}, u32[]{:S(2)}) copy-start(s32[512,1]{0,1:T(1,128)} %param.23) | copy-start | bytes 6148
  112.8 61.0 %copy-start.43 = (f32[768]{0:T(1024)}, f32[768]{0:T(1024)S(1)}, u32[]{:S(2)}) copy-start(f32[768]{0:T(1024)S(1)} %convert_element_type.104) | copy-start | bytes 9220
  173.8 154.5 %copy-start.7 = (f32[512,768]{1,0:T(8,128)}, f32[512,768]{1,0:T(8,128)S(1)}, u32[]{:S(2)}) copy-start(f32[512,768]{1,0:T(8,128)S(1)} %get-tuple-element.62) | copy-start | bytes 4718596
  173.8 2.2 copy-start.37
  195.6 10.3 %all-to-all-start.2 = ((bf16[8,8,768]{2,1,0:T(8,128)(2,1)}), bf16[8,8,768]{2,1,0:T(8,128)(2,1)}, u32[]{:S(2)}, u32[]{:S(2)}) async-start(bf16[8,8,768]{2,1,0:T(8,128)(2,1)} %get-tuple-element.68), calls=%async_computation.2 | async-start | bytes 196608 | tf_op jit(solution)/shard_map/all_to_all | solution.py:190
  209.6 15.2 %copy-start.38 = (s32[512,1]{0,1:T(1,128)S(1)}, s32[512,1]{0,1:T(1,128)}, u32[]{:S(2)}) copy-start(s32[512,1]{0,1:T(1,128)} %param.23) | copy-start | bytes 6148
  209.6 15.3 %copy-start.58 = (s32[512]{0:T(512)S(1)}, s32[512]{0:T(512)}, u32[]{:S(2)}) copy-start(s32[512]{0:T(512)} %copy-done.57) | copy-start | bytes 6148
  209.6 11.8 %all-to-all-start.3 = ((f32[8,8,768]{2,1,0:T(8,128)}), f32[8,8,768]{2,1,0:T(8,128)S(1)}, u32[]{:S(2)}, u32[]{:S(2)}) async-start(f32[8,8,768]{2,1,0:T(8,128)} %fusion.24), calls=%async_computation.3 | async-start | bytes 393216 | tf_op jit(solution)/shard_map/all_to_all | solution.py:196
  221.3 11.7 %all-to-all-start.1 = ((f32[8,8,768]{2,1,0:T(8,128)}), f32[8,8,768]{2,1,0:T(8,128)S(1)}, u32[]{:S(2)}, u32[]{:S(2)}) async-start(f32[8,8,768]{2,1,0:T(8,128)} %fusion.22), calls=%async_computation.1 | async-start | bytes 393216 | tf_op jit(solution)/shard_map/all_to_all | solution.py:179
  224.7 100.1 %all-reduce.17.cloned.1.call-start = ((), (), s32[]{:S(2)}) async-start(), calls=%async_computation.12 | async-start | bytes 6291456 | tf_op jit(solution)/shard_map/psum | solution.py:189
  233.0 2.6 copy-start.66
  239.4 85.5 %copy-start.13 = (bf16[512,768]{1,0:T(8,128)(2,1)S(1)}, bf16[512,768]{1,0:T(8,128)(2,1)}, u32[]{:S(2)}) copy-start(bf16[512,768]{1,0:T(8,128)(2,1)} %param.24) | copy-start | bytes 2359300
  239.4 87.1 %copy-start.53 = (f32[512]{0:T(512)S(1)}, f32[512]{0:T(512)}, u32[]{:S(2)}) copy-start(f32[512]{0:T(512)} %select_reduce_fusion.1) | copy-start | bytes 6148
  239.5 87.1 %copy-start.47 = (f32[512]{0:T(512)S(1)}, f32[512]{0:T(512)}, u32[]{:S(2)}) copy-start(f32[512]{0:T(512)} %copy-done.46) | copy-start | bytes 6148
  239.5 87.1 %copy-start.56 = (f32[512]{0:T(512)S(1)}, f32[512]{0:T(512)}, u32[]{:S(2)}) copy-start(f32[512]{0:T(512)} %copy-done.55) | copy-start | bytes 6148
  239.5 147.1 %reduce-scatter.14.cloned.1.call-start = ((), (), s32[]{:S(2)}) async-start(), calls=%async_computation.11 | async-start | bytes 442368
  324.9 3.4 copy-start.35
  324.9 3.4 copy-start.44
  324.9 3.4 copy-start.60
  328.3 3.4 copy-start.14
  328.3 3.4 copy-start.15
  328.3 3.4 copy-start.45
  328.3 3.4 copy-start.54
  328.3 3.4 copy-start.61
  331.7 4.2 copy-start.17
  331.7 4.6 copy-start.3
  336.3 63.3 %reduce-scatter.12.cloned.1.call-start = ((), (), s32[]{:S(2)}) async-start(), calls=%async_computation.10 | async-start | bytes 884736
  336.4 2.3 copy-start.5
  336.4 2.3 copy-start.26
  340.0 121.8 %all-reduce.15.cloned.1.call-start = ((), (), s32[]{:S(2)}) async-start(), calls=%async_computation.8 | async-start | bytes 3145728 | tf_op jit(solution)/shard_map/psum | solution.py:257
  340.1 2.8 copy-start.21
  347.7 151.9 %reduce-scatter.10.cloned.1.call-start = ((), (), s32[]{:S(2)}) async-start(), calls=%async_computation.9 | async-start | bytes 2211840
  350.6 3.0 copy-start.9
  382.9 3.3 copy-start.68
  382.9 79.0 %copy-start.12 = (bf16[512,768]{1,0:T(8,128)(2,1)S(1)}, bf16[512,768]{1,0:T(8,128)(2,1)}, u32[]{:S(2)}) copy-start(bf16[512,768]{1,0:T(8,128)(2,1)} %param.13) | copy-start | bytes 2359300
  386.2 77.7 %copy-start.64 = (f32[768]{0:T(1024)S(1)}, f32[768]{0:T(1024)}, u32[]{:S(2)}) copy-start(f32[768]{0:T(1024)} %get-tuple-element.50) | copy-start | bytes 9220
  386.2 107.7 %copy-start.6 = (f32[512,768]{1,0:T(8,128)S(1)}, f32[512,768]{1,0:T(8,128)}, u32[]{:S(2)}) copy-start(f32[512,768]{1,0:T(8,128)} %copy-done.4) | copy-start | bytes 4718596
  493.8 7.7 %copy-start.1 = (bf16[1,768,768]{2,1,0:T(8,128)(2,1)S(1)}, bf16[1,768,768]{2,1,0:T(8,128)(2,1)}, u32[]{:S(2)}) copy-start(bf16[1,768,768]{2,1,0:T(8,128)(2,1)} %param.20) | copy-start | bytes 3538948
  (36 other events, 47.4 us)
Sparse Core Ops, SparseCore 0:
  112.9 59.1 all-reduce.12
  239.6 85.2 all-reduce.16
  336.4 30.7 reduce-scatter.13
  370.0 29.5 reduce-scatter.11
  402.5 59.2 all-reduce.14
  464.2 35.4 reduce-scatter.9
where the time goes:
time: 516 us; the launch traced here: 509 us
  waiting for transfers between devices  218 us (42%)
  blocking collectives  104 us (20%)
  local copies, waits for them, and re-layouts  89.3 us (17%)
  matrix products  34.8 us (7%)
  other arithmetic  33.8 us (7%)
  between operations  17.5 us (3%)
  starting transfers between devices  11.4 us (2%)
    psum x1, waiting for transfers between devices, body(): expert_result = lax.psum(per_token, 'row')  84.1 us
    psum x1, waiting for transfers between devices, body(): lax.psum(jnp.einsum('ste,sde->td', grad_projected, full_qkv, preferred_el...  60.6 us
    unnamed x171, local copies, waits for them, and re-layouts  43 us
    psum x1, waiting for transfers between devices, body(): lax.psum(jnp.dot(heads_low, full_out, preferred_element_type=jnp.float32)...  42.6 us
    psum x1, blocking collectives, body(): table_grad = lax.psum(grad_table, ('exp', 'col'))  28.8 us
    all_gather x1, blocking collectives, body(): lax.all_gather(qkv_weight, ('exp', 'col'), axis=1, tiled=True)  22.2 us
    unnamed x1, blocking collectives  15.3 us
    unnamed x9, waiting for transfers between devices  14.6 us
  transfers between devices with their start and end apart: 9, of which 8 were waited for; matrix products, arithmetic and copies ran while one was open for 13% of the time, Pallas kernels for 0%

commit v1 on v0

v1 whole, which is shorter than its diff:
```python
import functools

import jax
import jax.numpy as jnp
import numpy as np
from jax import lax
from jax.experimental import pallas as pl
from jax.experimental.pallas import tpu as pltpu
from jax.sharding import PartitionSpec as P

DH = 64
CAP = 8
F32 = jnp.float32
BF16 = jnp.bfloat16
epsilon = 1e-06
thresholds = np.array([12, 16, 23, 32, 46, 64, 91], dtype=np.int32)
highest = lax.Precision.HIGHEST
MESH = pl.DeviceIdType.MESH
LIMIT = 56 * 1024 * 1024
VMEM = pl.BlockSpec(memory_space=pltpu.VMEM)
SMEM = pl.BlockSpec(memory_space=pltpu.SMEM)


def nt(a, b, precision=None):
    return lax.dot_general(
        a, b, (((1,), (1,)), ((), ())), preferred_element_type=F32, precision=precision
    )


def tn(a, b, precision=None):
    return lax.dot_general(
        a, b, (((0,), (0,)), ((), ())), preferred_element_type=F32, precision=precision
    )


def nn(a, b, precision=None):
    return jnp.dot(a, b, preferred_element_type=F32, precision=precision)


def call(kernel, outs, args, scratch=(), collective=None, specs=None):
    params = dict(vmem_limit_bytes=LIMIT)
    if collective is not None:
        params.update(collective_id=collective, has_side_effects=True)
    return pl.pallas_call(
        kernel,
        out_shape=[jax.ShapeDtypeStruct(s, d) for s, d in outs],
        in_specs=specs or [VMEM] * len(args),
        out_specs=[VMEM] * len(outs),
        scratch_shapes=list(scratch),
        compiler_params=pltpu.CompilerParams(**params),
    )(*args)


def enter(peers):
    barrier = pltpu.get_barrier_semaphore()
    for peer in peers:
        pl.semaphore_signal(barrier, inc=1, device_id=peer, device_id_type=MESH)
    pl.semaphore_wait(barrier, len(peers))


def remote(src, dst, send, recv, peer):
    copy = pltpu.make_async_remote_copy(
        src_ref=src, dst_ref=dst, send_sem=send, recv_sem=recv, device_id=peer, device_id_type=MESH
    )
    copy.start()
    return copy


def ring(axis, size):
    me = lax.axis_index(axis)
    return [lax.rem(me + k, size) for k in range(1, size)]


def group_peers(n_exp, n_col):
    n = n_exp * n_col
    me = lax.axis_index("exp") * n_col + lax.axis_index("col")
    return [lax.rem(me + k, n) for k in range(1, n)]


def gather_kernel(n_exp, w, s, w_all, s_all, send, recv, send_s, recv_s, c_send, c_recv, d_send, d_recv):
    e = lax.axis_index("exp")
    c = lax.axis_index("col")
    other = {"col": 1 - c}
    peers = ring("exp", n_exp)
    enter([{"exp": p} for p in peers] + [other])
    copies = []
    for k, p in enumerate(peers):
        copies.append(remote(s, s_all.at[e, c], send_s.at[k], recv_s.at[k], {"exp": p}))
        copies.append(remote(w, w_all.at[e, c], send.at[k], recv.at[k], {"exp": p}))
    last = [
        remote(s, s_all.at[e, c], d_send.at[0], d_recv.at[0], other),
        remote(w, w_all.at[e, c], c_send.at[0], c_recv.at[0], other),
    ]
    w_all[e, c] = w[...]
    s_all[e, c] = s[...]
    for k in range(n_exp - 1):
        q = lax.rem(e + n_exp - k - 1, n_exp)
        copies[2 * k].wait_recv()
        last.append(remote(s_all.at[q, c], s_all.at[q, c], d_send.at[k + 1], d_recv.at[k + 1], other))
        copies[2 * k + 1].wait_recv()
        last.append(remote(w_all.at[q, c], w_all.at[q, c], c_send.at[k + 1], c_recv.at[k + 1], other))
    for copy in copies:
        copy.wait_send()
    for copy in last:
        copy.wait()


def row_sum_kernel(n_row, x, out, held, send, recv, send2, recv2):
    r = lax.axis_index("row")
    peers = ring("row", n_row)
    enter([{"row": p} for p in peers])
    copies = [
        remote(x.at[p], held.at[k], send.at[k], recv.at[k], {"row": p}) for k, p in enumerate(peers)
    ]
    total = x[r].astype(F32)
    for k, copy in enumerate(copies):
        copy.wait_recv()
        total = total + held[k].astype(F32)
    out[r] = total.astype(BF16)
    more = [
        remote(out.at[r], out.at[r], send2.at[k], recv2.at[k], {"row": p})
        for k, p in enumerate(peers)
    ]
    for copy in copies:
        copy.wait_send()
    for copy in more:
        copy.wait()


def dispatch_kernel(n_exp, n_col, x, out, send, recv):
    me = lax.axis_index("exp") * n_col + lax.axis_index("col")
    peers = group_peers(n_exp, n_col)
    ids = [{"exp": p // n_col, "col": lax.rem(p, n_col)} for p in peers]
    enter(ids)
    copies = [
        remote(x.at[p], out.at[me], send.at[k], recv.at[k], ids[k]) for k, p in enumerate(peers)
    ]
    out[me] = x[me]
    for copy in copies:
        copy.wait()


def return_kernel(n_exp, n_col, n_row, x, out, held, total, send, recv, send2, recv2):
    n = n_exp * n_col
    share = n // n_row
    e = lax.axis_index("exp")
    c = lax.axis_index("col")
    r = lax.axis_index("row")
    me = e * n_col + c
    peers = ring("row", n_row)
    targets = []
    for g in range(share):
        for b in range(n_row):
            t = r * share + g
            targets.append((g, {"exp": t // n_col, "col": lax.rem(t, n_col), "row": b}))
    mine = me // share == r
    everyone = [
        (lax.rem(r + b, n_row), lax.rem(me + k, n))
        for b in range(n_row)
        for k in range(n)
        if b or k
    ]
    enter([{"exp": k // n_col, "col": lax.rem(k, n_col), "row": b} for b, k in everyone])
    copies = [
        remote(
            x.at[pl.ds(p * share, share)], held.at[k], send.at[k], recv.at[k], {"row": p}
        )
        for k, p in enumerate(peers)
    ]
    acc = x[pl.ds(r * share, share)].astype(F32)
    for k, copy in enumerate(copies):
        copy.wait_recv()
        acc = acc + held[k].astype(F32)
    total[...] = acc.astype(BF16)
    started = []
    for k, (g, target) in enumerate(targets):
        own = mine & (r * share + g == me) & (target["row"] == r)
        copy = pltpu.make_async_remote_copy(
            src_ref=total.at[g],
            dst_ref=out.at[me],
            send_sem=send2.at[k],
            recv_sem=recv2.at[me],
            device_id=target,
            device_id_type=MESH,
        )

        @pl.when(own)
        def _(g=g):
            out[me] = total[g]

        @pl.when(jnp.logical_not(own))
        def _(copy=copy):
            copy.start()

        started.append((own, copy))

    for own, copy in started:

        @pl.when(jnp.logical_not(own))
        def _(copy=copy):
            copy.wait_send()

    for copy in copies:
        copy.wait_send()
    for k in range(n):

        @pl.when(jnp.logical_not((k == me) & mine))
        def _(k=k):
            pltpu.make_async_remote_copy(
                src_ref=total.at[0],
                dst_ref=out.at[k],
                send_sem=send2.at[0],
                recv_sem=recv2.at[k],
                device_id={"row": r},
                device_id_type=MESH,
            ).wait_recv()


def final_kernel(
    n_exp, n_col, n_row, gw, sm, gh, tok, gm, gain,
    gt, gwo, smo,
    hrow, sib, pre, zheld, smheld, smrow,
    s_row, r_row, s_row2, r_row2, s_sib, r_sib, s_z, r_z, s_sm, r_sm, s_sm2, r_sm2,
):
    e = lax.axis_index("exp")
    c = lax.axis_index("col")
    r = lax.axis_index("row")
    me = e * n_col + c
    rows = ring("row", n_row)
    exps = ring("exp", n_exp)
    group = group_peers(n_exp, n_col)
    ids = [{"exp": p // n_col, "col": lax.rem(p, n_col)} for p in group]
    other = {"col": 1 - c}
    enter([{"row": p} for p in rows] + ids)
    sibling = remote(gw.at[1 - c], sib, s_sib, r_sib, other)
    row_copies = [
        remote(gh.at[p], hrow.at[k], s_row.at[k], r_row.at[k], {"row": p}) for k, p in enumerate(rows)
    ]
    small = [
        remote(sm.at[p], smheld.at[k], s_sm.at[k], r_sm.at[k], ids[k]) for k, p in enumerate(group)
    ]
    sibling.wait_recv()
    pre[...] = (gw[c].astype(F32) + sib[...].astype(F32)).astype(BF16)
    z_copies = [
        remote(pre.at[p], zheld.at[k], s_z.at[k], r_z.at[k], {"exp": p}) for k, p in enumerate(exps)
    ]
    part = sm[me]
    for k, copy in enumerate(small):
        copy.wait_recv()
        part = part + smheld[k]
    smrow[0] = part
    small2 = [
        remote(smrow.at[0], smrow.at[k + 1], s_sm2.at[k], r_sm2.at[k], {"row": p})
        for k, p in enumerate(rows)
    ]
    total = gh[r].astype(F32)
    for k, copy in enumerate(row_copies):
        copy.wait_recv()
        total = total + hrow[k].astype(F32)
    rows_in = tok[r].astype(F32)
    inv = lax.rsqrt(jnp.mean(rows_in * rows_in, axis=-1, keepdims=True) + epsilon)
    unit = rows_in * inv
    scaled = total * gain[...]
    grad = gm[r] + inv * (scaled - unit * jnp.mean(scaled * unit, axis=-1, keepdims=True))
    gt[r] = grad.astype(BF16)
    row_copies2 = [
        remote(gt.at[r], gt.at[r], s_row2.at[k], r_row2.at[k], {"row": p}) for k, p in enumerate(rows)
    ]
    full = part[9:10]
    for k, copy in enumerate(small2):
        copy.wait_recv()
        full = full + smrow[k + 1][9:10]
    row_at = lax.broadcasted_iota(jnp.int32, part.shape, 0)
    smo[...] = jnp.where(row_at == 9, jnp.broadcast_to(full, part.shape), part)
    wsum = pre[e].astype(F32)
    for k, copy in enumerate(z_copies):
        copy.wait_recv()
        wsum = wsum + zheld[k].astype(F32)
    gwo[...] = wsum
    for copy in [sibling] + row_copies + small + z_copies + small2:
        copy.wait_send()
    for copy in row_copies2:
        copy.wait()


def head_scores(q, k, rel_row, length, heads_at):
    size = q.shape[0]
    x = jnp.broadcast_to(rel_row, (size, 2 * size))
    bias = pltpu.roll(x, size + 1, 1, stride=1, stride_axis=0)[:, :size]
    scores = nt(q, k) * DH ** (-0.5) + bias
    key_at = lax.broadcasted_iota(jnp.int32, (1, size), 1)
    scores = jnp.where(key_at < length, scores, -1e30)
    top = jnp.max(scores, axis=-1, keepdims=True)
    raised = jnp.exp(scores - top)
    return raised * (1.0 / jnp.sum(raised, axis=-1, keepdims=True))


def forward_kernel(length, tok, w, gain, rel, hid, qkv, heads, attn):
    rows_in = tok[...].astype(F32)
    inv = lax.rsqrt(jnp.mean(rows_in * rows_in, axis=-1, keepdims=True) + epsilon)
    hid[...] = (rows_in * inv * gain[...]).astype(BF16)
    for m in range(3):
        qkv[m] = nn(hid[...], w[m]).astype(BF16)
    size = tok.shape[0]
    for h in range(qkv.shape[2] // DH):
        at = slice(h * DH, (h + 1) * DH)
        probs = head_scores(qkv[0, :, at], qkv[1, :, at], rel[h : h + 1], length[0], h)
        heads[:, at] = nn(probs.astype(BF16), qkv[2, :, at]).astype(BF16)
    attn[...] = nt(heads[...], w[3]).astype(BF16)


def middle(length, tok, attn, gain, router, route_row, route_col):
    size = tok.shape[0]
    experts = router.shape[0]
    mixed = tok[...].astype(F32) + attn[...].astype(F32)
    inv = lax.rsqrt(jnp.mean(mixed * mixed, axis=-1, keepdims=True) + epsilon)
    unit = mixed * inv
    hidden = (unit * gain[...]).astype(BF16)
    logits = nt(hidden, router[...])
    top = jnp.max(logits, axis=-1, keepdims=True)
    raised = jnp.exp(logits - top)
    probs = raised / jnp.sum(raised, axis=-1, keepdims=True)
    hot_col = lax.broadcasted_iota(jnp.int32, (size, experts), 1) == route_col[...]
    gate = jnp.sum(jnp.where(hot_col, probs, 0.0), axis=-1, keepdims=True)
    live = lax.broadcasted_iota(jnp.int32, (1, size), 1) < length
    hot = (lax.broadcasted_iota(jnp.int32, (experts, size), 0) == route_row[...]) & live
    hot = jnp.where(hot, 1.0, 0.0)
    earlier = jnp.where(
        lax.broadcasted_iota(jnp.int32, (size, size), 0)
        < lax.broadcasted_iota(jnp.int32, (size, size), 1),
        1.0,
        0.0,
    )
    before = nn(hot.astype(BF16), earlier.astype(BF16))
    rank = jnp.sum(hot * before, axis=0, keepdims=True).astype(jnp.int32)
    kept = live & (rank < CAP)
    target = jnp.where(kept, route_row[...] * CAP + rank, -1)
    match = lax.broadcasted_iota(jnp.int32, (experts * CAP, size), 0) == target
    match = jnp.where(match, 1.0, 0.0).astype(BF16)
    return mixed, inv, unit, hidden, probs, hot_col, gate, match


def send_kernel(length, tok, attn, gain, router, route_row, route_col, cot, out):
    _, _, _, hidden, _, _, gate, match = middle(
        length[0], tok, attn, gain, router, route_row, route_col
    )
    grad = (gate * cot[...].astype(F32)).astype(BF16)
    n = out.shape[0]
    first = nn(match, hidden).reshape(n, CAP, -1)
    second = nn(match, grad).reshape(n, CAP, -1)
    out[...] = jnp.concatenate([first, second], axis=1).astype(BF16)


def expert_kernel(x, w_in, w_out, part, grad_in, grad_out):
    n = x.shape[0]
    both = x[...].astype(F32)
    rows = both[:, :CAP].reshape(n * CAP, -1).astype(BF16)
    grads = both[:, CAP:].reshape(n * CAP, -1).astype(BF16)
    before = nn(rows, w_in[0])
    scale = np.float32(np.sqrt(2 / np.pi))
    inner = jnp.tanh(scale * (before + 0.044715 * before * before * before))
    acted = (0.5 * before * (1.0 + inner)).astype(BF16)
    slope = 0.5 * (1.0 + inner) + 0.5 * before * (1.0 - inner * inner) * scale * (
        1.0 + 3 * 0.044715 * before * before
    )
    result = nn(acted, w_out[0])
    grad_before = (slope * nt(grads, w_out[0])).astype(BF16)
    back = nt(grad_before, w_in[0])
    part[...] = jnp.concatenate(
        [result.reshape(n, CAP, -1), back.reshape(n, CAP, -1)], axis=1
    ).astype(BF16)
    grad_in[0] = tn(rows, grad_before)
    grad_out[0] = tn(acted, grads)


def backward_kernel(
    length, tok, attn, gain_two, router, route_row, route_col, cot, back, hid, qkv, heads, w, rel, picks,
    result, grad_mixed, gw, gh, small, table, gproj,
):
    mixed, inv, unit, hidden, probs, hot_col, gate, match = middle(
        length[0], tok, attn, gain_two, router, route_row, route_col
    )
    n = back.shape[0]
    size = tok.shape[0]
    both = back[...].astype(F32)
    out_rows = both[:, :CAP].reshape(n * CAP, -1).astype(BF16)
    back_rows = both[:, CAP:].reshape(n * CAP, -1).astype(BF16)
    expert_result = tn(match, out_rows)
    upstream = cot[...].astype(F32)
    result[...] = (mixed + gate * expert_result).astype(BF16)
    grad_gate = jnp.sum(upstream * expert_result, axis=-1, keepdims=True)
    grad_logits = probs * (jnp.where(hot_col, grad_gate, 0.0) - gate * grad_gate)
    grad_low = grad_logits.astype(BF16)
    grad_rest = (grad_logits - grad_low.astype(F32)).astype(BF16)
    small[0 : router.shape[0]] = tn(grad_low, hidden) + tn(grad_rest, hidden)
    grad_hidden = tn(match, back_rows) + nn(grad_low, router[...]) + nn(grad_rest, router[...])
    small[router.shape[0] : router.shape[0] + 1] = jnp.sum(grad_hidden * unit, axis=0, keepdims=True)
    scaled = grad_hidden * gain_two[...]
    gm = upstream + inv * (scaled - unit * jnp.mean(scaled * unit, axis=-1, keepdims=True))
    grad_mixed[...] = gm
    gattn = gm.astype(BF16)
    gw[3] = tn(gattn, heads[...]).astype(BF16)
    grad_heads = nn(gattn, w[3]).astype(BF16)
    flip = jnp.where(
        lax.broadcasted_iota(jnp.int32, (size, size), 0)
        + lax.broadcasted_iota(jnp.int32, (size, size), 1)
        == size - 1,
        1.0,
        0.0,
    ).astype(BF16)
    for h in range(qkv.shape[2] // DH):
        at = slice(h * DH, (h + 1) * DH)
        q, k, v = qkv[0, :, at], qkv[1, :, at], qkv[2, :, at]
        probs_full = head_scores(q, k, rel[h : h + 1], length[0], h)
        gheads = grad_heads[:, at]
        gprobs = nt(gheads, v)
        dot = jnp.sum(probs_full * gprobs, axis=-1, keepdims=True)
        gscores = (probs_full * (gprobs - dot)).astype(BF16)
        gproj[2, :, at] = tn(probs_full.astype(BF16), gheads).astype(BF16)
        gproj[0, :, at] = (nn(gscores, k) * DH ** (-0.5)).astype(BF16)
        gproj[1, :, at] = (tn(gscores, q) * DH ** (-0.5)).astype(BF16)
        turned = nn(flip, gscores)
        turned = jnp.concatenate([turned, jnp.zeros((size, size), F32)], axis=1)
        turned = pltpu.roll(turned, 0, 1, stride=1, stride_axis=0)
        diagonal = jnp.sum(turned, axis=0, keepdims=True)
        table[h : h + 1] = nn(diagonal, picks[...], highest)
    ghid = jnp.zeros(tok.shape, F32)
    for m in range(3):
        gw[m] = tn(hid[...], gproj[m]).astype(BF16)
        ghid = ghid + nt(gproj[m], w[m])
    gh[...] = ghid.astype(BF16)
    rows_in = tok[...].astype(F32)
    unit_one = rows_in * lax.rsqrt(jnp.mean(rows_in * rows_in, axis=-1, keepdims=True) + epsilon)
    small[router.shape[0] + 1 : router.shape[0] + 2] = jnp.sum(ghid * unit_one, axis=0, keepdims=True)


def bucket_picks(length, buckets):
    offset = np.arange(2 * length) - (length - 1)
    distance = np.abs(offset)
    beyond = np.sum(distance[:, None] >= thresholds, axis=-1)
    bucket = (offset > 0) * 16 + np.minimum(distance, 8) + beyond
    return (bucket[:, None] == np.arange(buckets)[None, :]).astype(np.float32)


def body(
    n_exp, n_col, n_row,
    tokens, qkv_weight, out_weight, bias_table, gain_attn, gain_expert, router_weight,
    expert_in, expert_out, lengths, routes, cotangent,
):
    n = n_exp * n_col
    size, width = tokens.shape
    shard = width // n
    local = qkv_weight.shape[2]
    heads_local = local // DH
    experts = router_weight.shape[1]
    lines = -(-(experts + 2) // 16) * 16
    dma = lambda k: pltpu.SemaphoreType.DMA((k,))
    packed = jnp.concatenate([qkv_weight, out_weight.T[None]], axis=0)
    small = jnp.concatenate(
        [router_weight.T, gain_attn[None], gain_expert[None]], axis=0
    )
    small = jnp.pad(small, ((0, lines - experts - 2), (0, 128 - shard)))
    w_all, s_all = call(
        functools.partial(gather_kernel, n_exp),
        [((n_exp, n_col) + packed.shape, BF16), ((n_exp, n_col) + small.shape, BF16)],
        [packed, small],
        [dma(n_exp - 1)] * 4 + [dma(n_exp)] * 4,
        1,
    )
    w = w_all.reshape(n, 4, shard, local).transpose(1, 0, 2, 3).reshape(4, width, local)
    s = s_all.reshape(n, lines, 128)[:, :, :shard].transpose(1, 0, 2).reshape(lines, width)
    router = s[:experts]
    gain_one = s[experts : experts + 1].astype(F32)
    gain_two = s[experts + 1 : experts + 2].astype(F32)
    picks = bucket_picks(size, bias_table.shape[0])
    rel = jnp.dot(
        bias_table.T, jnp.asarray(picks.T, BF16), preferred_element_type=F32
    )
    route_row = routes.reshape(1, size)
    hid, qkv, heads, attn_part = call(
        forward_kernel,
        [((size, width), BF16), ((3, size, local), BF16), ((size, local), BF16), ((size, width), BF16)],
        [lengths, tokens, w, gain_one, rel],
        specs=[SMEM] + [VMEM] * 4,
    )
    block = size // n_row
    (attn,) = call(
        functools.partial(row_sum_kernel, n_row),
        [((n_row, block, width), BF16)],
        [attn_part.reshape(n_row, block, width)],
        [pltpu.VMEM((n_row - 1, block, width), BF16)] + [dma(n_row - 1)] * 4,
        2,
    )
    attn = attn.reshape(size, width)
    (sent,) = call(
        send_kernel,
        [((n, 2 * CAP, width), BF16)],
        [lengths, tokens, attn, gain_two, router, route_row, routes, cotangent],
        specs=[SMEM] + [VMEM] * 7,
    )
    (arrived,) = call(
        functools.partial(dispatch_kernel, n_exp, n_col),
        [((n, 2 * CAP, width), BF16)],
        [sent],
        [dma(n - 1)] * 2,
        3,
    )
    part, grad_expert_in, grad_expert_out = call(
        expert_kernel,
        [((n, 2 * CAP, width), BF16), (expert_in.shape, F32), (expert_out.shape, F32)],
        [arrived, expert_in, expert_out],
    )
    share = n // n_row
    (back,) = call(
        functools.partial(return_kernel, n_exp, n_col, n_row),
        [((n, 2 * CAP, width), BF16)],
        [part],
        [
            pltpu.VMEM((n_row - 1, share, 2 * CAP, width), BF16),
            pltpu.VMEM((share, 2 * CAP, width), BF16),
            dma(n_row - 1),
            dma(n_row - 1),
            dma(share * n_row),
            dma(n),
        ],
        4,
    )
    result, grad_mixed, gw, gh, grads, table = call(
        backward_kernel,
        [
            ((size, width), BF16),
            ((size, width), F32),
            ((4, width, local), BF16),
            ((size, width), BF16),
            ((lines, width), F32),
            ((heads_local, bias_table.shape[0]), F32),
        ],
        [
            lengths, tokens, attn, gain_two, router, route_row, routes, cotangent, back,
            hid, qkv, heads, w, rel, jnp.asarray(picks),
        ],
        [pltpu.VMEM((3, size, local), BF16)],
        specs=[SMEM] + [VMEM] * 14,
    )
    gw = gw.reshape(4, n_exp, n_col, shard, local).transpose(2, 1, 0, 3, 4)
    lead = jnp.concatenate(
        [grads[:8], grads[experts : experts + 2], grads[8:experts]], axis=0
    )
    lead = lead.reshape(experts + 2, n, shard).transpose(1, 0, 2)
    lead = jnp.pad(lead, ((0, 0), (0, lines - experts - 2), (0, 128 - shard)))
    tail = jnp.pad(table, ((0, 8 - heads_local), (0, 128 - table.shape[1])))
    lead = jnp.concatenate([lead, jnp.broadcast_to(tail[None], (n, 8, 128))], axis=1)
    high = lines + 8
    gt, gwo, smo = call(
        functools.partial(final_kernel, n_exp, n_col, n_row),
        [((n_row, block, width), BF16), ((4, shard, local), F32), ((high, 128), F32)],
        [
            gw, lead, gh.reshape(n_row, block, width), tokens.reshape(n_row, block, width),
            grad_mixed.reshape(n_row, block, width), gain_one,
        ],
        [
            pltpu.VMEM((n_row - 1, block, width), BF16),
            pltpu.VMEM((n_exp, 4, shard, local), BF16),
            pltpu.VMEM((n_exp, 4, shard, local), BF16),
            pltpu.VMEM((n_exp - 1, 4, shard, local), BF16),
            pltpu.VMEM((n - 1, high, 128), F32),
            pltpu.VMEM((n_row, high, 128), F32),
            dma(n_row - 1), dma(n_row - 1), dma(n_row - 1), dma(n_row - 1),
            pltpu.SemaphoreType.DMA, pltpu.SemaphoreType.DMA,
            dma(n_exp - 1), dma(n_exp - 1),
            dma(n - 1), dma(n - 1), dma(n_row - 1), dma(n_row - 1),
        ],
        5,
    )
    grad_router = jnp.concatenate([smo[:8], smo[10 : experts + 2]], axis=0)[:, :shard].T
    return (
        result,
        gt.reshape(size, width),
        gwo[:3],
        gwo[3].T,
        smo[lines : lines + heads_local, : bias_table.shape[0]].T,
        smo[9, :shard],
        smo[8, :shard],
        grad_router,
        grad_expert_in,
        grad_expert_out,
    )


def solution(mesh):
    both = ("exp", "col")
    placed = (
        P(both, None),
        P(None, both, "row"),
        P("row", both),
        P(None, "row"),
        P(both),
        P(both),
        P(both, None),
        P(both, None, "row"),
        P(both, "row", None),
        P(both),
        P(both, None),
        P(both, None),
    )
    shape = mesh.shape
    return jax.shard_map(
        functools.partial(body, shape["exp"], shape["col"], shape["row"]),
        mesh=mesh,
        in_specs=placed,
        out_specs=(
            P(both, None),
            P(both, None),
            P(None, both, "row"),
            P("row", both),
            P(None, "row"),
            P(both),
            P(both),
            P(both, None),
            P(both, None, "row"),
            P(both, "row", None),
        ),
        check_vma=False,
    )
```

time: 516 us -> 169 us (0.33); the launches traced: 509 us -> 168 us
  waiting for transfers between devices: 218 us -> 0 us
  Pallas kernels: 0 us -> 142 us
  blocking collectives: 104 us -> 0 us
  local copies, waits for them, and re-layouts: 89.3 us -> 19.1 us
  matrix products: 34.8 us -> 1.56 us
  other arithmetic: 33.8 us -> 3.6 us
  between operations: 17.5 us -> 1.43 us
  starting transfers between devices: 11.4 us -> 0 us
    psum x3 -> x0, waiting for transfers between devices: 187 us -> none  [the longest x1 84.1 us: body(): expert_result = lax.psum(per_token, 'row')]
    pallas_call x0 -> x9, Pallas kernels: none -> 142 us  [call(): pl.pallas_call(kernel, out_shape=[jax.ShapeDtypeStruct(s, d) for s, d in...]
    all_gather x3 -> x0, blocking collectives: 49.4 us -> none  [the longest x1 22.2 us: body(): lax.all_gather(qkv_weight, ('exp', 'col'), axis=1, tiled=True)]
    unnamed x171 -> x13, local copies, waits for them, and re-layouts: 43 us -> 5.26 us
    psum x1 -> x0, blocking collectives: 28.8 us -> none  [body(): table_grad = lax.psum(grad_table, ('exp', 'col'))]
    dot_general x20 -> x1, matrix products: 29.9 us -> 1.56 us  [body(): jnp.dot(bias_table.T, jnp.asarray(picks.T, BF16), preferred_element_type=...]
    all_to_all x3 -> x0, waiting for transfers between devices: 15.9 us -> none  [the longest x1 5.87 us: body(): lax.all_to_all(grad_arrived_in.reshape(groups * local_experts, CAP, model...]
    unnamed x1 -> x0, blocking collectives: 15.3 us -> none
  transfers between devices with their start and end apart: 9 -> 0, of which waited for: 8 -> 0; matrix products, arithmetic and copies ran while one was open for 13% -> 0% of each run, Pallas kernels for 0% -> 0%
where the time goes in v1:
time: 169 us; the launch traced here: 168 us
  Pallas kernels  142 us (84%)
  local copies, waits for them, and re-layouts  19.1 us (11%)
  other arithmetic  3.6 us (2%)
    pallas_call x9, Pallas kernels, call(): pl.pallas_call(kernel, out_shape=[jax.ShapeDtypeStruct(s, d) for s, d in...  142 us
    unnamed x13, local copies, waits for them, and re-layouts  5.26 us

profile of v1, /device:TPU:0, one launch (start us, length us, event | category | flops | bytes accessed | tf_op | source)
XLA Modules:
  0.0 167.9 jit_solution(2935644660401406978)
XLA Ops:
  0.6 0.0 copy-start
  1.3 1.3 fusion.8.s
  2.6 0.0 copy-done
  2.6 1.6 convolution_bitcast_fusion.rel
  4.2 0.9 copy.30
  5.1 1.6 pad_maximum_fusion.w
  6.7 1.5 copy.34.route_col
  8.3 23.2 %shard_map.213 = (bf16[4,2,4,96,192]{4,3,2,1,0:T(8,128)(2,1)}, bf16[4,2,16,128]{3,2,1,0:T(8,128)(2,1)}) custom-call(bf16[4,96,192]{2,1,0:T(8,128)(2,1)} %pad_maximum_fusion.w, bf16[16,128]{1,0:T(8,128)(2,1)} %fusion.8.s), custom_call_target="tpu_custom_call" | custom-call | tf_op jit(solution)/shard_map/pallas_call | solution.py:44
  31.4 0.0 copy-start.2
  31.4 2.7 %copy.31 = bf16[8,4,96,192]{3,2,0,1:T(8,128)(2,1)} copy(bf16[8,4,96,192]{3,2,1,0:T(8,128)(2,1)} %bitcast.54) | data formatting | bytes 2359296 | tf_op jit(solution)/shard_map/reshape | solution.py:470
  34.1 0.0 copy-done.2
  34.2 0.7 slice.44.router
  34.8 0.7 reshape.102.gain.gain_two
  35.5 0.7 reshape.101.gain
  36.2 6.4 %shard_map.214 = (bf16[512,768]{1,0:T(8,128)(2,1)}, bf16[3,512,192]{2,1,0:T(8,128)(2,1)}, bf16[512,192]{1,0:T(8,128)(2,1)}, bf16[512,768]{1,0:T(8,128)(2,1)}) custom-call(s32[1]{0:T(128)S(6)} %copy.49.length, bf16[512,768]{1,0:T(8,128)(2,1)} %tok.5, bf16[4,768,192]{2,1,0:T(8,128)(2,1)} %bitcast.46, f32[1,768]{1,0:T(1,128)} %reshape.101.gain, ...), custom_call_target="tpu_custom_call" | custom-call | tf_op jit(solution)/shard_map/pallas_call | solution.py:44
  42.6 25.4 %shard_map.215 = bf16[4,128,768]{2,1,0:T(8,128)(2,1)} custom-call(bf16[4,128,768]{2,1,0:T(8,128)(2,1)} %bitcast.57), custom_call_target="tpu_custom_call" | custom-call | tf_op jit(solution)/shard_map/pallas_call | solution.py:44
  68.0 3.8 %shard_map.216.x = bf16[8,16,768]{2,1,0:T(8,128)(2,1)} custom-call(s32[1]{0:T(128)S(6)} %copy.49.length, bf16[512,768]{1,0:T(8,128)(2,1)} %tok.5, bf16[512,768]{1,0:T(8,128)(2,1)} %bitcast.49, f32[1,768]{1,0:T(1,128)} %reshape.102.gain.gain_two, bf16[8,768]{1,0:T(8,128)(2,1)} %slice.44.router, s32[1,512]{1,0:T(1,128)} %bitcast.64, s32[512,1]{1,0:T(8,128)} %copy.34.route_col, ...), custom_call_target="tpu_custom_call" | custom-call | tf_op jit(solution)/shard_map/pallas_call | solution.py:44
  71.8 11.9 %shard_map.217.x = bf16[8,16,768]{2,1,0:T(8,128)(2,1)} custom-call(bf16[8,16,768]{2,1,0:T(8,128)(2,1)} %shard_map.216.x), custom_call_target="tpu_custom_call" | custom-call | tf_op jit(solution)/shard_map/pallas_call | solution.py:44
  83.7 5.5 %shard_map.218 = (bf16[8,16,768]{2,1,0:T(8,128)(2,1)}, f32[1,768,768]{2,1,0:T(8,128)}, f32[1,768,768]{2,1,0:T(8,128)}) custom-call(bf16[8,16,768]{2,1,0:T(8,128)(2,1)} %shard_map.217.x, bf16[1,768,768]{2,1,0:T(8,128)(2,1)} %w_in.1, bf16[1,768,768]{2,1,0:T(8,128)(2,1)} %w_out.1), custom_call_target="tpu_custom_call" | custom-call | tf_op jit(solution)/shard_map/pallas_call | solution.py:44
  89.2 21.3 %shard_map.219.back = bf16[8,16,768]{2,1,0:T(8,128)(2,1)} custom-call(bf16[8,16,768]{2,1,0:T(8,128)(2,1)} %get-tuple-element.31.x), custom_call_target="tpu_custom_call" | custom-call | tf_op jit(solution)/shard_map/pallas_call | solution.py:44
  110.5 14.4 %shard_map.220 = (bf16[512,768]{1,0:T(8,128)(2,1)}, f32[512,768]{1,0:T(8,128)}, bf16[4,768,192]{2,1,0:T(8,128)(2,1)}, bf16[512,768]{1,0:T(8,128)(2,1)}, f32[16,768]{1,0:T(8,128)}, /*index=5*/f32[3,32]{1,0:T(4,128)}) custom-call(s32[1]{0:T(128)S(6)} %copy.49.length, bf16[512,768]{1,0:T(8,128)(2,1)} %tok.5, bf16[512,768]{1,0:T(8,128)(2,1)} %bitcast.50, ...), custom_call_target="tpu_custom_call" | custom-call | tf_op jit(solution)/shard_map/pallas_call | solution.py:44
  124.9 0.0 copy-start.3
  124.9 0.0 copy-start.1
  124.9 2.7 %copy.45 = bf16[4,4,2,96,192]{4,3,0,1,2:T(8,128)(2,1)} copy(bf16[4,4,2,96,192]{4,3,2,1,0:T(8,128)(2,1)} %bitcast.53) | data formatting | bytes 2359296 | tf_op jit(solution)/shard_map/reshape | solution.py:545
  127.7 0.0 copy-done.3
  127.7 0.0 copy-done.1
  127.7 0.1 reshape.96
  127.8 0.7 select_maximum_fusion.sm
  128.4 30.3 %shard_map.221 = (bf16[4,128,768]{2,1,0:T(8,128)(2,1)}, f32[4,96,192]{2,1,0:T(8,128)}, f32[24,128]{1,0:T(8,128)}) custom-call(bf16[2,4,4,96,192]{4,3,2,1,0:T(8,128)(2,1)} %bitcast.51, f32[8,24,128]{2,1,0:T(8,128)} %select_maximum_fusion.sm, bf16[4,128,768]{2,1,0:T(8,128)(2,1)} %bitcast.55, bf16[4,128,768]{2,1,0:T(8,128)(2,1)} %bitcast.48, ...), custom_call_target="tpu_custom_call" | custom-call | tf_op jit(solution)/shard_map/pallas_call | solution.py:44
  158.8 1.3 slice_bitcast_fusion.3
  160.0 1.3 slice_bitcast_fusion.2
  161.3 1.3 slice_bitcast_fusion.1
  162.5 0.9 slice_bitcast_fusion
  163.4 1.7 %slice.45 = f32[3,96,192]{2,1,0:T(8,128)} slice(f32[4,96,192]{2,1,0:T(8,128)} %get-tuple-element.42), slice={[0:3], [0:96], [0:192]} | slice | bytes 442368 | tf_op jit(solution)/shard_map/slice | solution.py:579
  165.1 0.7 copy.38
  165.9 2.1 %copy.50 = bf16[512,768]{1,0:T(8,128)(2,1)} copy(bf16[512,768]{1,0:T(8,128)(2,1)} %bitcast.56) | data formatting | bytes 1572864
  (6 shorter events, 0.0 us)
Async XLA Ops:
  0.6 2.0 %copy-start = (bf16[32,3]{0,1:T(4,128)(2,1)S(1)}, bf16[32,3]{0,1:T(4,128)(2,1)}, u32[]{:S(2)}) copy-start(bf16[32,3]{0,1:T(4,128)(2,1)} %param.17) | copy-start | bytes 580
  31.4 2.7 %copy-start.2 = (bf16[4,2,16,128]{3,2,1,0:T(8,128)(2,1)S(1)}, bf16[4,2,16,128]{3,2,1,0:T(8,128)(2,1)}, u32[]{:S(2)}) copy-start(bf16[4,2,16,128]{3,2,1,0:T(8,128)(2,1)} %get-tuple-element.29) | copy-start | bytes 98308
  124.9 2.7 %copy-start.3 = (f32[3,32]{1,0:T(4,128)S(1)}, f32[3,32]{1,0:T(4,128)}, u32[]{:S(2)}) copy-start(f32[3,32]{1,0:T(4,128)} %get-tuple-element.38) | copy-start | bytes 1156
  124.9 2.7 %copy-start.1 = (f32[16,768]{1,0:T(8,128)S(1)}, f32[16,768]{1,0:T(8,128)}, u32[]{:S(2)}) copy-start(f32[16,768]{1,0:T(8,128)} %get-tuple-element.37) | copy-start | bytes 147460

commit v2 on v1

v2 whole, which is shorter than its diff:
```python
import functools

import jax
import jax.numpy as jnp
import numpy as np
from jax import lax
from jax.experimental import pallas as pl
from jax.experimental.pallas import tpu as pltpu
from jax.sharding import PartitionSpec as P

DH = 64
CAP = 8
F32 = jnp.float32
BF16 = jnp.bfloat16
epsilon = 1e-06
thresholds = np.array([12, 16, 23, 32, 46, 64, 91], dtype=np.int32)
highest = lax.Precision.HIGHEST
MESH = pl.DeviceIdType.MESH
LIMIT = 56 * 1024 * 1024
VMEM = pl.BlockSpec(memory_space=pltpu.VMEM)
SMEM = pl.BlockSpec(memory_space=pltpu.SMEM)


def nt(a, b, precision=None):
    return lax.dot_general(
        a, b, (((1,), (1,)), ((), ())), preferred_element_type=F32, precision=precision
    )


def tn(a, b, precision=None):
    return lax.dot_general(
        a, b, (((0,), (0,)), ((), ())), preferred_element_type=F32, precision=precision
    )


def nn(a, b, precision=None):
    return jnp.dot(a, b, preferred_element_type=F32, precision=precision)


def call(kernel, outs, args, scratch=(), collective=None, specs=None):
    params = dict(vmem_limit_bytes=LIMIT)
    if collective is not None:
        params.update(collective_id=collective, has_side_effects=True)
    return pl.pallas_call(
        kernel,
        out_shape=[jax.ShapeDtypeStruct(s, d) for s, d in outs],
        in_specs=specs or [VMEM] * len(args),
        out_specs=[VMEM] * len(outs),
        scratch_shapes=list(scratch),
        compiler_params=pltpu.CompilerParams(**params),
    )(*args)


def greet(peers):
    barrier = pltpu.get_barrier_semaphore()
    for peer in peers:
        pl.semaphore_signal(barrier, inc=1, device_id=peer, device_id_type=MESH)


def meet(peers):
    pl.semaphore_wait(pltpu.get_barrier_semaphore(), len(peers))


def enter(peers):
    greet(peers)
    meet(peers)


def remote(src, dst, send, recv, peer):
    copy = pltpu.make_async_remote_copy(
        src_ref=src, dst_ref=dst, send_sem=send, recv_sem=recv, device_id=peer, device_id_type=MESH
    )
    copy.start()
    return copy


def ring(axis, size):
    me = lax.axis_index(axis)
    return [lax.rem(me + k, size) for k in range(1, size)]


def group_peers(n_exp, n_col):
    n = n_exp * n_col
    me = lax.axis_index("exp") * n_col + lax.axis_index("col")
    return [lax.rem(me + k, n) for k in range(1, n)]


def gather_kernel(n_exp, w, s, w_all, s_all, send, recv, send_s, recv_s, c_send, c_recv, d_send, d_recv):
    e = lax.axis_index("exp")
    c = lax.axis_index("col")
    other = {"col": 1 - c}
    peers = ring("exp", n_exp)
    enter([{"exp": p} for p in peers] + [other])
    copies = []
    for k, p in enumerate(peers):
        copies.append(remote(s, s_all.at[e, c], send_s.at[k], recv_s.at[k], {"exp": p}))
        copies.append(remote(w, w_all.at[e, c], send.at[k], recv.at[k], {"exp": p}))
    last = [
        remote(s, s_all.at[e, c], d_send.at[0], d_recv.at[0], other),
        remote(w, w_all.at[e, c], c_send.at[0], c_recv.at[0], other),
    ]
    w_all[e, c] = w[...]
    s_all[e, c] = s[...]
    for k in range(n_exp - 1):
        q = lax.rem(e + n_exp - k - 1, n_exp)
        copies[2 * k].wait_recv()
        last.append(remote(s_all.at[q, c], s_all.at[q, c], d_send.at[k + 1], d_recv.at[k + 1], other))
        copies[2 * k + 1].wait_recv()
        last.append(remote(w_all.at[q, c], w_all.at[q, c], c_send.at[k + 1], c_recv.at[k + 1], other))
    for copy in copies:
        copy.wait_send()
    for copy in last:
        copy.wait()


def bias_grid(rel_row, size):
    x = jnp.broadcast_to(rel_row, (size, 2 * size))
    return pltpu.roll(x, size + 1, 1, stride=1, stride_axis=0)[:, :size]


def head_probs(q, k, bias, length):
    scores = nt(q, k) * DH ** (-0.5) + bias
    key_at = lax.broadcasted_iota(jnp.int32, (1, k.shape[0]), 1)
    scores = jnp.where(key_at < length, scores, -1e30)
    top = jnp.max(scores, axis=-1, keepdims=True)
    raised = jnp.exp(scores - top)
    return raised * (1.0 / jnp.sum(raised, axis=-1, keepdims=True))


def forward_kernel(
    n_row, length, tok, w_in, gain, rel,
    w, hid, qkv, heads, out,
    bias, x, held, send, recv, send2, recv2,
):
    r = lax.axis_index("row")
    peers = ring("row", n_row)
    ids = [{"row": p} for p in peers]
    greet(ids)
    size = tok.shape[0]
    block = size // n_row
    local = qkv.shape[2]
    if len(w_in.shape) == 3:
        w[...] = w_in[...]
    else:
        _, n_col, _, shard, _ = w_in.shape
        for e in range(w_in.shape[0]):
            for c in range(n_col):
                at = (e * n_col + c) * shard
                w[:, at : at + shard] = w_in[e, c]
    rows_in = tok[...].astype(F32)
    inv = lax.rsqrt(jnp.mean(rows_in * rows_in, axis=-1, keepdims=True) + epsilon)
    hid[...] = (rows_in * inv * gain[...]).astype(BF16)
    for m in range(3):
        qkv[m] = nn(hid[...], w[m]).astype(BF16)
    for h in range(local // DH):
        bias[h] = bias_grid(rel[h : h + 1], size)
    copies = []
    for k, p in enumerate(peers + [r]):
        rows = pl.ds(pl.multiple_of(p * block, block), block)
        for h in range(local // DH):
            at = slice(h * DH, (h + 1) * DH)
            probs = head_probs(qkv[0, rows, at], qkv[1, :, at], bias[h, rows], length[0])
            heads[rows, at] = nn(probs.astype(BF16), qkv[2, :, at]).astype(BF16)
        x[k] = nt(heads[rows, :], w[3]).astype(BF16)
        if k == 0:
            meet(ids)
        if k < n_row - 1:
            copies.append(remote(x.at[k], held.at[k], send.at[k], recv.at[k], {"row": p}))
    total = x[n_row - 1].astype(F32)
    for k, copy in enumerate(copies):
        copy.wait_recv()
        total = total + held[k].astype(F32)
    out[r] = total.astype(BF16)
    more = [
        remote(out.at[r], out.at[r], send2.at[k], recv2.at[k], {"row": p})
        for k, p in enumerate(peers)
    ]
    for copy in copies:
        copy.wait_send()
    for copy in more:
        copy.wait()


def middle(length, tok, attn, gain, router, route_row, route_col):
    size = tok.shape[0]
    experts = router.shape[0]
    mixed = tok[...].astype(F32) + attn[...].astype(F32)
    inv = lax.rsqrt(jnp.mean(mixed * mixed, axis=-1, keepdims=True) + epsilon)
    unit = mixed * inv
    hidden = (unit * gain[...]).astype(BF16)
    logits = nt(hidden, router[...])
    top = jnp.max(logits, axis=-1, keepdims=True)
    raised = jnp.exp(logits - top)
    probs = raised / jnp.sum(raised, axis=-1, keepdims=True)
    hot_col = lax.broadcasted_iota(jnp.int32, (size, experts), 1) == route_col[...]
    gate = jnp.sum(jnp.where(hot_col, probs, 0.0), axis=-1, keepdims=True)
    live = lax.broadcasted_iota(jnp.int32, (1, size), 1) < length
    hot = (lax.broadcasted_iota(jnp.int32, (experts, size), 0) == route_row[...]) & live
    hot = jnp.where(hot, 1.0, 0.0)
    earlier = jnp.where(
        lax.broadcasted_iota(jnp.int32, (size, size), 0)
        < lax.broadcasted_iota(jnp.int32, (size, size), 1),
        1.0,
        0.0,
    )
    before = nn(hot.astype(BF16), earlier.astype(BF16))
    rank = jnp.sum(hot * before, axis=0, keepdims=True).astype(jnp.int32)
    kept = live & (rank < CAP)
    target = jnp.where(kept, route_row[...] * CAP + rank, -1)
    match = lax.broadcasted_iota(jnp.int32, (experts * CAP, size), 0) == target
    match = jnp.where(match, 1.0, 0.0).astype(BF16)
    return mixed, inv, unit, hidden, probs, hot_col, gate, match


def expert_kernel(
    n_exp, n_col, n_row,
    length, tok, attn, gain, router, route_row, route_col, cot, w_in, w_out,
    out, rows, grads, acted, grad_before,
    sent, arrived, part, held, total, send0, recv0, send, recv, send2, recv2,
):
    n = n_exp * n_col
    share = n // n_row
    r = lax.axis_index("row")
    me = lax.axis_index("exp") * n_col + lax.axis_index("col")
    mine = me // share == r
    everyone = [
        (lax.rem(r + b, n_row), lax.rem(me + k, n))
        for b in range(n_row)
        for k in range(n)
        if b or k
    ]
    everyone = [{"exp": k // n_col, "col": lax.rem(k, n_col), "row": b} for b, k in everyone]
    greet(everyone)
    _, _, _, hidden, _, _, gate, match = middle(
        length[0], tok, attn, gain, router, route_row, route_col
    )
    grad = (gate * cot[...].astype(F32)).astype(BF16)
    first = nn(match, hidden).reshape(n, CAP, -1)
    second = nn(match, grad).reshape(n, CAP, -1)
    sent[...] = jnp.concatenate([first, second], axis=1).astype(BF16)
    meet(everyone)
    group = group_peers(n_exp, n_col)
    copies = [
        remote(
            sent.at[p],
            arrived.at[me],
            send0.at[k],
            recv0.at[k],
            {"exp": p // n_col, "col": lax.rem(p, n_col)},
        )
        for k, p in enumerate(group)
    ]
    arrived[me] = sent[me]
    for copy in copies:
        copy.wait()
    both = arrived[...].astype(F32)
    rows[...] = both[:, :CAP].reshape(n * CAP, -1).astype(BF16)
    grads[...] = both[:, CAP:].reshape(n * CAP, -1).astype(BF16)
    before = nn(rows[...], w_in[0])
    scale = np.float32(np.sqrt(2 / np.pi))
    inner = jnp.tanh(scale * (before + 0.044715 * before * before * before))
    acted[...] = (0.5 * before * (1.0 + inner)).astype(BF16)
    slope = 0.5 * (1.0 + inner) + 0.5 * before * (1.0 - inner * inner) * scale * (
        1.0 + 3 * 0.044715 * before * before
    )
    result = nn(acted[...], w_out[0])
    grad_before[...] = (slope * nt(grads[...], w_out[0])).astype(BF16)
    back = nt(grad_before[...], w_in[0])
    part[...] = jnp.concatenate(
        [result.reshape(n, CAP, -1), back.reshape(n, CAP, -1)], axis=1
    ).astype(BF16)
    copies = [
        remote(part.at[pl.ds(p * share, share)], held.at[k], send.at[k], recv.at[k], {"row": p})
        for k, p in enumerate(ring("row", n_row))
    ]
    acc = part[pl.ds(r * share, share)].astype(F32)
    for k, copy in enumerate(copies):
        copy.wait_recv()
        acc = acc + held[k].astype(F32)
    total[...] = acc.astype(BF16)
    started = []
    for g in range(share):
        for b in range(n_row):
            t = r * share + g
            own = mine & (t == me) & (r == b)
            copy = pltpu.make_async_remote_copy(
                src_ref=total.at[g],
                dst_ref=out.at[me],
                send_sem=send2.at[g * n_row + b],
                recv_sem=recv2.at[me],
                device_id={"exp": t // n_col, "col": lax.rem(t, n_col), "row": b},
                device_id_type=MESH,
            )

            @pl.when(own)
            def _(g=g):
                out[me] = total[g]

            @pl.when(jnp.logical_not(own))
            def _(copy=copy):
                copy.start()

            started.append((own, copy))

    for own, copy in started:

        @pl.when(jnp.logical_not(own))
        def _(copy=copy):
            copy.wait_send()

    for copy in copies:
        copy.wait_send()
    for k in range(n):

        @pl.when(jnp.logical_not((k == me) & mine))
        def _(k=k):
            pltpu.make_async_remote_copy(
                src_ref=total.at[0],
                dst_ref=out.at[k],
                send_sem=send2.at[0],
                recv_sem=recv2.at[k],
                device_id={"row": r},
                device_id_type=MESH,
            ).wait_recv()


def expert_grad_kernel(rows, grads, acted, grad_before, grad_in, grad_out):
    grad_in[0] = tn(rows[...], grad_before[...])
    grad_out[0] = tn(acted[...], grads[...])


def backward_kernel(
    n_exp, n_col, n_row,
    length, tok, attn, gain_one, gain_two, router, route_row, route_col, cot, back, hid, qkv, heads,
    w, rel, picks,
    result, gt, gwo, smo,
    gproj, gw, gm, gh, sm, hrow, sib, pre, zheld, smheld, smrow,
    s_row, r_row, s_row2, r_row2, s_sib, r_sib, s_z, r_z, s_sm, r_sm, s_sm2, r_sm2,
):
    e = lax.axis_index("exp")
    c = lax.axis_index("col")
    r = lax.axis_index("row")
    n = n_exp * n_col
    me = e * n_col + c
    rows = ring("row", n_row)
    exps = ring("exp", n_exp)
    group = group_peers(n_exp, n_col)
    ids = [{"exp": p // n_col, "col": lax.rem(p, n_col)} for p in group]
    everyone = [{"row": p} for p in rows] + ids
    greet(everyone)
    size, width = tok.shape
    block = size // n_row
    shard = width // n
    experts = router.shape[0]
    local = qkv.shape[2]

    def place(m, grad):
        for k in range(n):
            gw[k % n_col, k // n_col, m] = grad[k * shard : (k + 1) * shard].astype(BF16)

    mixed, inv, unit, hidden, probs, hot_col, gate, match = middle(
        length[0], tok, attn, gain_two, router, route_row, route_col
    )
    both = back[...].astype(F32)
    out_rows = both[:, :CAP].reshape(n * CAP, -1).astype(BF16)
    back_rows = both[:, CAP:].reshape(n * CAP, -1).astype(BF16)
    expert_result = tn(match, out_rows)
    upstream = cot[...].astype(F32)
    result[...] = (mixed + gate * expert_result).astype(BF16)
    grad_gate = jnp.sum(upstream * expert_result, axis=-1, keepdims=True)
    grad_logits = probs * (jnp.where(hot_col, grad_gate, 0.0) - gate * grad_gate)
    grad_low = grad_logits.astype(BF16)
    grad_rest = (grad_logits - grad_low.astype(F32)).astype(BF16)
    grad_router = tn(grad_low, hidden) + tn(grad_rest, hidden)
    grad_hidden = tn(match, back_rows) + nn(grad_low, router[...]) + nn(grad_rest, router[...])
    grad_gain_two = jnp.sum(grad_hidden * unit, axis=0, keepdims=True)
    scaled = grad_hidden * gain_two[...]
    gm[...] = upstream + inv * (scaled - unit * jnp.mean(scaled * unit, axis=-1, keepdims=True))
    gattn = gm[...].astype(BF16)
    place(3, tn(gattn, heads[...]))
    grad_heads = nn(gattn, w[3]).astype(BF16)
    flip = jnp.where(
        lax.broadcasted_iota(jnp.int32, (size, size), 0)
        + lax.broadcasted_iota(jnp.int32, (size, size), 1)
        == size - 1,
        1.0,
        0.0,
    ).astype(BF16)
    sm[...] = jnp.zeros(sm.shape, F32)
    lines = experts + 2
    for h in range(local // DH):
        at = slice(h * DH, (h + 1) * DH)
        q, k, v = qkv[0, :, at], qkv[1, :, at], qkv[2, :, at]
        probs_full = head_probs(q, k, bias_grid(rel[h : h + 1], size), length[0])
        gheads = grad_heads[:, at]
        gprobs = nt(gheads, v)
        dot = jnp.sum(probs_full * gprobs, axis=-1, keepdims=True)
        gscores = (probs_full * (gprobs - dot)).astype(BF16)
        gproj[2, :, at] = tn(probs_full.astype(BF16), gheads).astype(BF16)
        gproj[0, :, at] = (nn(gscores, k) * DH ** (-0.5)).astype(BF16)
        gproj[1, :, at] = (tn(gscores, q) * DH ** (-0.5)).astype(BF16)
        turned = nn(flip, gscores)
        turned = jnp.concatenate([turned, jnp.zeros((size, size), F32)], axis=1)
        turned = pltpu.roll(turned, 0, 1, stride=1, stride_axis=0)
        diagonal = jnp.sum(turned, axis=0, keepdims=True)
        line = nn(diagonal, picks[...], highest)
        for k in range(n):
            sm[k, lines + h : lines + h + 1, 0 : line.shape[1]] = line
    row_copies = []
    grad_gain_one = jnp.zeros((1, width), F32)
    for k, p in enumerate(rows + [r]):
        at = pl.ds(pl.multiple_of(p * block, block), block)
        ghid = nt(gproj[0, at, :], w[0]) + nt(gproj[1, at, :], w[1]) + nt(gproj[2, at, :], w[2])
        rows_in = tok[at, :].astype(F32)
        inv_one = lax.rsqrt(jnp.mean(rows_in * rows_in, axis=-1, keepdims=True) + epsilon)
        unit_one = rows_in * inv_one
        grad_gain_one = grad_gain_one + jnp.sum(ghid * unit_one, axis=0, keepdims=True)
        if k == 0:
            meet(everyone)
        if k < n_row - 1:
            gh[k] = ghid.astype(BF16)
            row_copies.append(remote(gh.at[k], hrow.at[k], s_row.at[k], r_row.at[k], {"row": p}))
    for m in range(3):
        place(m, tn(hid[...], gproj[m]))
    sibling = remote(gw.at[1 - c], sib, s_sib, r_sib, {"col": 1 - c})
    for k in range(n):
        at = slice(k * shard, (k + 1) * shard)
        sm[k, 0:experts, 0:shard] = grad_router[:, at]
        sm[k, experts : experts + 1, 0:shard] = grad_gain_two[:, at]
        sm[k, experts + 1 : experts + 2, 0:shard] = grad_gain_one[:, at]
    small = [
        remote(sm.at[p], smheld.at[k], s_sm.at[k], r_sm.at[k], ids[k]) for k, p in enumerate(group)
    ]
    sibling.wait_recv()
    pre[...] = (gw[c].astype(F32) + sib[...].astype(F32)).astype(BF16)
    z_copies = [
        remote(pre.at[p], zheld.at[k], s_z.at[k], r_z.at[k], {"exp": p}) for k, p in enumerate(exps)
    ]
    total = ghid
    for k, copy in enumerate(row_copies):
        copy.wait_recv()
        total = total + hrow[k].astype(F32)
    scaled = total * gain_one[...]
    own = pl.ds(pl.multiple_of(r * block, block), block)
    gt[r] = (
        gm[own, :]
        + inv_one * (scaled - unit_one * jnp.mean(scaled * unit_one, axis=-1, keepdims=True))
    ).astype(BF16)
    row_copies2 = [
        remote(gt.at[r], gt.at[r], s_row2.at[k], r_row2.at[k], {"row": p}) for k, p in enumerate(rows)
    ]
    part = sm[me]
    for k, copy in enumerate(small):
        copy.wait_recv()
        part = part + smheld[k]
    smrow[0] = part
    small2 = [
        remote(smrow.at[0], smrow.at[k + 1], s_sm2.at[k], r_sm2.at[k], {"row": p})
        for k, p in enumerate(rows)
    ]
    full = part
    for k, copy in enumerate(small2):
        copy.wait_recv()
        full = full + smrow[k + 1]
    row_at = lax.broadcasted_iota(jnp.int32, part.shape, 0)
    smo[...] = jnp.where(row_at == experts + 1, full, part)
    wsum = pre[e].astype(F32)
    for k, copy in enumerate(z_copies):
        copy.wait_recv()
        wsum = wsum + zheld[k].astype(F32)
    gwo[...] = wsum
    for copy in [sibling] + row_copies + small + z_copies + small2:
        copy.wait_send()
    for copy in row_copies2:
        copy.wait()


def bucket_picks(length, buckets):
    offset = np.arange(2 * length) - (length - 1)
    distance = np.abs(offset)
    beyond = np.sum(distance[:, None] >= thresholds, axis=-1)
    bucket = (offset > 0) * 16 + np.minimum(distance, 8) + beyond
    return (bucket[:, None] == np.arange(buckets)[None, :]).astype(np.float32)


def body(
    n_exp, n_col, n_row,
    tokens, qkv_weight, out_weight, bias_table, gain_attn, gain_expert, router_weight,
    expert_in, expert_out, lengths, routes, cotangent,
):
    n = n_exp * n_col
    size, width = tokens.shape
    shard = width // n
    local = qkv_weight.shape[2]
    heads_local = local // DH
    experts = router_weight.shape[1]
    lines = -(-(experts + 2) // 16) * 16
    dma = lambda k: pltpu.SemaphoreType.DMA((k,))
    packed = jnp.concatenate([qkv_weight, out_weight.T[None]], axis=0)
    small = jnp.concatenate(
        [router_weight.T, gain_attn[None], gain_expert[None]], axis=0
    )
    small = jnp.pad(small, ((0, lines - experts - 2), (0, 128 - shard)))
    w_all, s_all = call(
        functools.partial(gather_kernel, n_exp),
        [((n_exp, n_col) + packed.shape, BF16), ((n_exp, n_col) + small.shape, BF16)],
        [packed, small],
        [dma(n_exp - 1)] * 4 + [dma(n_exp)] * 4,
        1,
    )
    if shard % 16:
        w_all = w_all.reshape(n, 4, shard, local).transpose(1, 0, 2, 3).reshape(4, width, local)
    s = s_all.reshape(n, lines, 128)[:, :, :shard].transpose(1, 0, 2).reshape(lines, width)
    router = s[:experts]
    gain_one = s[experts : experts + 1].astype(F32)
    gain_two = s[experts + 1 : experts + 2].astype(F32)
    picks = bucket_picks(size, bias_table.shape[0])
    rel = jnp.dot(
        bias_table.T, jnp.asarray(picks.T, BF16), preferred_element_type=F32
    )
    route_row = routes.reshape(1, size)
    block = size // n_row
    w, hid, qkv, heads, attn = call(
        functools.partial(forward_kernel, n_row),
        [
            ((4, width, local), BF16),
            ((size, width), BF16),
            ((3, size, local), BF16),
            ((size, local), BF16),
            ((n_row, block, width), BF16),
        ],
        [lengths, tokens, w_all, gain_one, rel],
        [
            pltpu.VMEM((heads_local, size, size), F32),
            pltpu.VMEM((n_row, block, width), BF16),
            pltpu.VMEM((n_row - 1, block, width), BF16),
        ]
        + [dma(n_row - 1)] * 4,
        2,
        specs=[SMEM] + [VMEM] * 4,
    )
    attn = attn.reshape(size, width)
    share = n // n_row
    slots = pltpu.VMEM((n, 2 * CAP, width), BF16)
    back, *saved = call(
        functools.partial(expert_kernel, n_exp, n_col, n_row),
        [
            ((n, 2 * CAP, width), BF16),
            ((n * CAP, width), BF16),
            ((n * CAP, width), BF16),
            ((n * CAP, expert_in.shape[2]), BF16),
            ((n * CAP, expert_in.shape[2]), BF16),
        ],
        [
            lengths, tokens, attn, gain_two, router, route_row, routes, cotangent, expert_in,
            expert_out,
        ],
        [
            slots, slots, slots,
            pltpu.VMEM((n_row - 1, share, 2 * CAP, width), BF16),
            pltpu.VMEM((share, 2 * CAP, width), BF16),
            dma(n - 1), dma(n - 1), dma(n_row - 1), dma(n_row - 1), dma(share * n_row), dma(n),
        ],
        3,
        specs=[SMEM] + [VMEM] * 9,
    )
    grad_expert_in, grad_expert_out = call(
        expert_grad_kernel, [(expert_in.shape, F32), (expert_out.shape, F32)], saved
    )
    high = -(-(experts + 2 + heads_local) // 8) * 8
    result, gt, gwo, smo = call(
        functools.partial(backward_kernel, n_exp, n_col, n_row),
        [
            ((size, width), BF16),
            ((n_row, block, width), BF16),
            ((4, shard, local), F32),
            ((high, 128), F32),
        ],
        [
            lengths, tokens, attn, gain_one, gain_two, router, route_row, routes, cotangent, back,
            hid, qkv, heads, w, rel, jnp.asarray(picks),
        ],
        [
            pltpu.VMEM((3, size, local), BF16),
            pltpu.VMEM((n_col, n_exp, 4, shard, local), BF16),
            pltpu.VMEM((size, width), F32),
            pltpu.VMEM((n_row - 1, block, width), BF16),
            pltpu.VMEM((n, high, 128), F32),
            pltpu.VMEM((n_row - 1, block, width), BF16),
            pltpu.VMEM((n_exp, 4, shard, local), BF16),
            pltpu.VMEM((n_exp, 4, shard, local), BF16),
            pltpu.VMEM((n_exp - 1, 4, shard, local), BF16),
            pltpu.VMEM((n - 1, high, 128), F32),
            pltpu.VMEM((n_row, high, 128), F32),
            dma(n_row - 1), dma(n_row - 1), dma(n_row - 1), dma(n_row - 1),
            pltpu.SemaphoreType.DMA, pltpu.SemaphoreType.DMA,
            dma(n_exp - 1), dma(n_exp - 1),
            dma(n - 1), dma(n - 1), dma(n_row - 1), dma(n_row - 1),
        ],
        4,
        specs=[SMEM] + [VMEM] * 15,
    )
    lines = experts + 2
    return (
        result,
        gt.reshape(size, width),
        gwo[:3],
        gwo[3].T,
        smo[lines : lines + heads_local, : bias_table.shape[0]].T,
        smo[experts + 1, :shard],
        smo[experts, :shard],
        smo[:experts, :shard].T,
        grad_expert_in,
        grad_expert_out,
    )


def solution(mesh):
    both = ("exp", "col")
    placed = (
        P(both, None),
        P(None, both, "row"),
        P("row", both),
        P(None, "row"),
        P(both),
        P(both),
        P(both, None),
        P(both, None, "row"),
        P(both, "row", None),
        P(both),
        P(both, None),
        P(both, None),
    )
    shape = mesh.shape
    return jax.shard_map(
        functools.partial(body, shape["exp"], shape["col"], shape["row"]),
        mesh=mesh,
        in_specs=placed,
        out_specs=(
            P(both, None),
            P(both, None),
            P(None, both, "row"),
            P("row", both),
            P(None, "row"),
            P(both),
            P(both),
            P(both, None),
            P(both, None, "row"),
            P(both, "row", None),
        ),
        check_vma=False,
    )
```

time: 169 us -> 148 us (0.88)
  Pallas kernels: 142 us -> 126 us
  local copies, waits for them, and re-layouts: 19.1 us -> 15.3 us
    pallas_call x9 -> x5, Pallas kernels: 142 us -> 126 us  [call(): pl.pallas_call(kernel, out_shape=[jax.ShapeDtypeStruct(s, d) for s, d in...]
    reshape x4 -> x0, local copies, waits for them, and re-layouts: 5.48 us -> none  [the longest x1 2.7 us: body(): gw = gw.reshape(4, n_exp, n_col, shard, local).transpose(2, 1, 0, 3, 4)]
    unnamed x13 -> x10, local copies, waits for them, and re-layouts: 5.26 us -> 6.88 us
where the time goes in v2:
time: 148 us; the launch traced here: 147 us
  Pallas kernels  126 us (85%)
  local copies, waits for them, and re-layouts  15.3 us (10%)
  other arithmetic  2.95 us (2%)
  matrix products  1.57 us (1%)
    pallas_call x5, Pallas kernels, call(): pl.pallas_call(kernel, out_shape=[jax.ShapeDtypeStruct(s, d) for s, d in...  126 us
    unnamed x10, local copies, waits for them, and re-layouts  6.88 us

profile of v2, /device:TPU:0, one launch (start us, length us, event | category | flops | bytes accessed | tf_op | source)
XLA Modules:
  0.0 147.0 jit_solution(15380981479749106051)
XLA Ops:
  0.6 0.0 copy-start
  1.3 1.3 fusion.8.s
  2.6 0.0 copy-done
  2.6 1.6 %convolution_bitcast_fusion.rel = f32[3,1024]{1,0:T(4,128)} fusion(bf16[32,1024]{1,0:T(8,128)(2,1)} %constant.7.clone, bf16[32,3]{0,1:T(4,128)(2,1)S(1)} %copy-done), kind=kOutput, calls=%fused_computation | convolution fusion | flops 196608 | bytes 78016 | tf_op jit(solution)/shard_map/dot_general | solution.py:518
  4.2 0.9 copy.24
  5.1 1.6 %pad_maximum_fusion.w = bf16[4,96,192]{2,1,0:T(8,128)(2,1)} fusion(bf16[1,96,192]{2,1,0:T(8,128)(2,1)S(1)} %bitcast.33, bf16[3,96,192]{2,1,0:T(8,128)(2,1)} %param.15), kind=kLoop, calls=%fused_computation.1 | loop fusion | flops 73728 | bytes 294912 | tf_op jit(solution)/shard_map/concatenate | solution.py:499
  6.7 1.5 %copy.27.route_col = s32[512,1]{1,0:T(8,128)} copy(s32[512,1]{0,1:T(1,128)} %param.24) | data formatting | bytes 4096 | tf_op args[10]
  8.3 23.2 %shard_map.213 = (bf16[4,2,4,96,192]{4,3,2,1,0:T(8,128)(2,1)}, bf16[4,2,16,128]{3,2,1,0:T(8,128)(2,1)}) custom-call(bf16[4,96,192]{2,1,0:T(8,128)(2,1)} %pad_maximum_fusion.w, bf16[16,128]{1,0:T(8,128)(2,1)} %fusion.8.s), custom_call_target="tpu_custom_call" | custom-call | tf_op jit(solution)/shard_map/pallas_call | solution.py:44
  31.4 0.8 copy.31
  32.2 0.7 slice.39.router
  32.9 0.7 reshape.69.gain.gain_two
  33.6 0.7 reshape.68.gain.gain_one
  34.2 29.5 %shard_map.214 = (bf16[4,768,192]{2,1,0:T(8,128)(2,1)}, bf16[512,768]{1,0:T(8,128)(2,1)}, bf16[3,512,192]{2,1,0:T(8,128)(2,1)}, bf16[512,192]{1,0:T(8,128)(2,1)}, bf16[4,128,768]{2,1,0:T(8,128)(2,1)}) custom-call(s32[1]{0:T(128)S(6)} %copy.34.length, bf16[512,768]{1,0:T(8,128)(2,1)} %tok.5, bf16[4,2,4,96,192]{4,3,2,1,0:T(8,128)(2,1)} %get-tuple-element.28.w_in, ...), custom_call_target="tpu_custom_call" | custom-call | tf_op jit(solution)/shard_map/pallas_call | solution.py:44
  63.7 31.6 %shard_map.215 = (bf16[8,16,768]{2,1,0:T(8,128)(2,1)}, bf16[64,768]{1,0:T(8,128)(2,1)}, bf16[64,768]{1,0:T(8,128)(2,1)}, bf16[64,768]{1,0:T(8,128)(2,1)}, bf16[64,768]{1,0:T(8,128)(2,1)}) custom-call(s32[1]{0:T(128)S(6)} %copy.34.length, bf16[512,768]{1,0:T(8,128)(2,1)} %tok.5, bf16[512,768]{1,0:T(8,128)(2,1)} %bitcast.30, f32[1,768]{1,0:T(1,128)} %reshape.69.gain.gain_two, ...), custom_call_target="tpu_custom_call" | custom-call | tf_op jit(solution)/shard_map/pallas_call | solution.py:44
  95.3 37.8 %shard_map.216 = (bf16[512,768]{1,0:T(8,128)(2,1)}, bf16[4,128,768]{2,1,0:T(8,128)(2,1)}, f32[4,96,192]{2,1,0:T(8,128)}, f32[16,128]{1,0:T(8,128)}) custom-call(s32[1]{0:T(128)S(6)} %copy.34.length, bf16[512,768]{1,0:T(8,128)(2,1)} %tok.5, bf16[512,768]{1,0:T(8,128)(2,1)} %bitcast.31, f32[1,768]{1,0:T(1,128)} %reshape.68.gain.gain_one, ...), custom_call_target="tpu_custom_call" | custom-call | tf_op jit(solution)/shard_map/pallas_call | solution.py:44
  133.1 0.0 copy-start.1
  133.1 1.3 slice_bitcast_fusion.3
  134.4 1.3 slice_bitcast_fusion.2
  135.7 1.3 slice_bitcast_fusion.1
  136.9 0.9 slice_bitcast_fusion
  137.8 1.7 %slice.40 = f32[3,96,192]{2,1,0:T(8,128)} slice(f32[4,96,192]{2,1,0:T(8,128)} %get-tuple-element.38), slice={[0:3], [0:96], [0:192]} | slice | bytes 442368 | tf_op jit(solution)/shard_map/slice | solution.py:607
  139.5 0.7 copy.28
  140.3 3.8 %shard_map.217 = (f32[1,768,768]{2,1,0:T(8,128)}, f32[1,768,768]{2,1,0:T(8,128)}) custom-call(bf16[64,768]{1,0:T(8,128)(2,1)} %get-tuple-element.40.rows, bf16[64,768]{1,0:T(8,128)(2,1)} %get-tuple-element.41.grads, bf16[64,768]{1,0:T(8,128)(2,1)} %get-tuple-element.42.acted, bf16[64,768]{1,0:T(8,128)(2,1)} %get-tuple-element.43.grad_before), custom_call_target="tpu_custom_call" | custom-call | tf_op jit(solution)/shard_map/pallas_call | solution.py:44
  144.1 2.1 %copy.35 = bf16[512,768]{1,0:T(8,128)(2,1)} copy(bf16[512,768]{1,0:T(8,128)(2,1)} %get-tuple-element.70) | data formatting | bytes 1572864
  146.1 0.0 copy-done.1
  146.1 0.9 copy.36
  (2 shorter events, 0.0 us)
Async XLA Ops:
  0.6 2.0 %copy-start = (bf16[32,3]{0,1:T(4,128)(2,1)S(1)}, bf16[32,3]{0,1:T(4,128)(2,1)}, u32[]{:S(2)}) copy-start(bf16[32,3]{0,1:T(4,128)(2,1)} %param.17) | copy-start | bytes 580
  133.1 13.0 %copy-start.1 = (bf16[4,128,768]{2,1,0:T(8,128)(2,1)S(1)}, bf16[4,128,768]{2,1,0:T(8,128)(2,1)}, u32[]{:S(2)}) copy-start(bf16[4,128,768]{2,1,0:T(8,128)(2,1)} %get-tuple-element.37) | copy-start | bytes 2359300

commit v3 on v2

v3 whole, which is shorter than its diff:
```python
import functools

import jax
import jax.numpy as jnp
import numpy as np
from jax import lax
from jax.experimental import pallas as pl
from jax.experimental.pallas import tpu as pltpu
from jax.sharding import PartitionSpec as P

DH = 64
CAP = 8
F32 = jnp.float32
BF16 = jnp.bfloat16
epsilon = 1e-06
thresholds = np.array([12, 16, 23, 32, 46, 64, 91], dtype=np.int32)
highest = lax.Precision.HIGHEST
MESH = pl.DeviceIdType.MESH
LIMIT = 56 * 1024 * 1024
VMEM = pl.BlockSpec(memory_space=pltpu.VMEM)
SMEM = pl.BlockSpec(memory_space=pltpu.SMEM)


def nt(a, b, precision=None):
    return lax.dot_general(
        a, b, (((1,), (1,)), ((), ())), preferred_element_type=F32, precision=precision
    )


def tn(a, b, precision=None):
    return lax.dot_general(
        a, b, (((0,), (0,)), ((), ())), preferred_element_type=F32, precision=precision
    )


def nn(a, b, precision=None):
    return jnp.dot(a, b, preferred_element_type=F32, precision=precision)


def call(kernel, outs, args, scratch=(), collective=None, specs=None):
    params = dict(vmem_limit_bytes=LIMIT)
    if collective is not None:
        params.update(collective_id=collective, has_side_effects=True)
    return pl.pallas_call(
        kernel,
        out_shape=[jax.ShapeDtypeStruct(s, d) for s, d in outs],
        in_specs=specs or [VMEM] * len(args),
        out_specs=[VMEM] * len(outs),
        scratch_shapes=list(scratch),
        compiler_params=pltpu.CompilerParams(**params),
    )(*args)


def greet(peers):
    barrier = pltpu.get_barrier_semaphore()
    for peer in peers:
        pl.semaphore_signal(barrier, inc=1, device_id=peer, device_id_type=MESH)


def meet(peers):
    pl.semaphore_wait(pltpu.get_barrier_semaphore(), len(peers))


def enter(peers):
    greet(peers)
    meet(peers)


def remote(src, dst, send, recv, peer):
    copy = pltpu.make_async_remote_copy(
        src_ref=src, dst_ref=dst, send_sem=send, recv_sem=recv, device_id=peer, device_id_type=MESH
    )
    copy.start()
    return copy


def ring(axis, size):
    me = lax.axis_index(axis)
    return [lax.rem(me + k, size) for k in range(1, size)]


def group_peers(n_exp, n_col):
    n = n_exp * n_col
    me = lax.axis_index("exp") * n_col + lax.axis_index("col")
    return [lax.rem(me + k, n) for k in range(1, n)]


def bias_grid(rel_row, size):
    x = jnp.broadcast_to(rel_row, (size, 2 * size))
    return pltpu.roll(x, size + 1, 1, stride=1, stride_axis=0)[:, :size]


def head_probs(q, k, bias, length):
    scores = nt(q, k) * DH ** (-0.5) + bias
    key_at = lax.broadcasted_iota(jnp.int32, (1, k.shape[0]), 1)
    scores = jnp.where(key_at < length, scores, -1e30)
    top = jnp.max(scores, axis=-1, keepdims=True)
    raised = jnp.exp(scores - top)
    return raised * (1.0 / jnp.sum(raised, axis=-1, keepdims=True))


def eye(size, dtype=BF16):
    return jnp.where(
        lax.broadcasted_iota(jnp.int32, (size, size), 0)
        == lax.broadcasted_iota(jnp.int32, (size, size), 1),
        1.0,
        0.0,
    ).astype(dtype)


def forward_kernel(
    n_exp, n_col, n_row,
    length, tok, w_own, out_own, gain_one, gain_two, router, table, picks,
    w, hid, qkv, heads, out, vectors, rel,
    bias, x, held, small, small_all, w_all, o_own, o_all,
    send, recv, send2, recv2, s_w, r_w, s_o, r_o, s_s, r_s, c_w, d_w, c_o, d_o, c_s, d_s,
):
    e = lax.axis_index("exp")
    c = lax.axis_index("col")
    r = lax.axis_index("row")
    peers = ring("row", n_row)
    exps = ring("exp", n_exp)
    other = {"col": 1 - c}
    everyone = [{"row": p} for p in peers] + [{"exp": p} for p in exps] + [other]
    greet(everyone)
    size = tok.shape[0]
    block = size // n_row
    local = qkv.shape[2]
    shard = w_own.shape[1]
    experts = router.shape[1]
    small[...] = jnp.zeros(small.shape, F32)
    small[0:experts, 0:shard] = tn(router[...], eye(shard))
    small[experts : experts + 1, 0:shard] = gain_one[...].astype(F32)
    small[experts + 1 : experts + 2, 0:shard] = gain_two[...].astype(F32)
    o_own[...] = nt(eye(shard), out_own[...]).astype(BF16)
    small_all[e, c] = small[...]
    w_all[e, c] = w_own[...]
    o_all[e, c] = o_own[...]
    meet(everyone)
    gathers = [
        (small, small_all, s_s, r_s, c_s, d_s),
        (w_own, w_all, s_w, r_w, c_w, d_w),
        (o_own, o_all, s_o, r_o, c_o, d_o),
    ]
    first = [
        [
            remote(own, full.at[e, c], a.at[k], b.at[k], {"exp": p})
            for own, full, a, b, _, _ in gathers
        ]
        for k, p in enumerate(exps)
    ]
    second = [
        [remote(own, full.at[e, c], a.at[0], b.at[0], other)] for own, full, _, _, a, b in gathers
    ]

    def forward_on(which):
        _, full, _, _, a, b = gathers[which]
        for k in range(n_exp - 1):
            q = lax.rem(e + n_exp - k - 1, n_exp)
            first[k][which].wait_recv()
            at = full.at[q, c]
            second[which].append(remote(at, at, a.at[k + 1], b.at[k + 1], other))

    rel[...] = tn(table[...], picks[...])
    for h in range(local // DH):
        bias[h] = bias_grid(rel[h : h + 1], size)
    rows_in = tok[...].astype(F32)
    inv = lax.rsqrt(jnp.mean(rows_in * rows_in, axis=-1, keepdims=True) + epsilon)
    forward_on(0)
    forward_on(1)
    for which in range(2):
        for copy in second[which]:
            copy.wait_recv()
    for k in range(n_exp * n_col):
        at = slice(k * shard, (k + 1) * shard)
        vectors[:, at] = small_all[k // n_col, k % n_col][:, :shard]
        if shard % 16 == 0:
            w[0:3, at] = w_all[k // n_col, k % n_col]
    if shard % 16:
        pieces = [
            w_all[k // n_col, k % n_col].astype(F32) for k in range(n_exp * n_col)
        ]
        w[0:3] = jnp.concatenate(pieces, axis=1).astype(BF16)
    hid[...] = (rows_in * inv * vectors[experts : experts + 1]).astype(BF16)
    for m in range(3):
        qkv[m] = nn(hid[...], w[m]).astype(BF16)
    forward_on(2)
    copies = []
    for k, p in enumerate(peers + [r]):
        rows = pl.ds(pl.multiple_of(p * block, block), block)
        for h in range(local // DH):
            at = slice(h * DH, (h + 1) * DH)
            probs = head_probs(qkv[0, rows, at], qkv[1, :, at], bias[h, rows], length[0])
            heads[rows, at] = nn(probs.astype(BF16), qkv[2, :, at]).astype(BF16)
        if k == 0:
            for copy in second[2]:
                copy.wait_recv()
            if shard % 16:
                pieces = [
                    o_all[j // n_col, j % n_col].astype(F32) for j in range(n_exp * n_col)
                ]
                w[3] = jnp.concatenate(pieces, axis=0).astype(BF16)
            else:
                for j in range(n_exp * n_col):
                    w[3, j * shard : (j + 1) * shard] = o_all[j // n_col, j % n_col]
        x[k] = nt(heads[rows, :], w[3]).astype(BF16)
        if k < n_row - 1:
            copies.append(remote(x.at[k], held.at[k], send.at[k], recv.at[k], {"row": p}))
    total = x[n_row - 1].astype(F32)
    for k, copy in enumerate(copies):
        copy.wait_recv()
        total = total + held[k].astype(F32)
    out[r] = total.astype(BF16)
    more = [
        remote(out.at[r], out.at[r], send2.at[k], recv2.at[k], {"row": p})
        for k, p in enumerate(peers)
    ]
    for copy in copies + sum(first, []) + sum(second, []):
        copy.wait_send()
    for copy in more:
        copy.wait()


def middle(length, tok, attn, vectors, experts, route_row):
    size = tok.shape[0]
    mixed = tok[...].astype(F32) + attn[...].astype(F32)
    inv = lax.rsqrt(jnp.mean(mixed * mixed, axis=-1, keepdims=True) + epsilon)
    unit = mixed * inv
    hidden = (unit * vectors[experts + 1 : experts + 2]).astype(BF16)
    logits = nt(hidden, vectors[0:experts].astype(BF16))
    top = jnp.max(logits, axis=-1, keepdims=True)
    raised = jnp.exp(logits - top)
    probs = raised / jnp.sum(raised, axis=-1, keepdims=True)
    live = lax.broadcasted_iota(jnp.int32, (1, size), 1) < length
    chosen = lax.broadcasted_iota(jnp.int32, (experts, size), 0) == route_row[...]
    chosen = jnp.where(chosen, 1.0, 0.0)
    hot_col = tn(chosen.astype(BF16), eye(experts))
    gate = jnp.sum(hot_col * probs, axis=-1, keepdims=True)
    hot = jnp.where(live, chosen, 0.0)
    earlier = jnp.where(
        lax.broadcasted_iota(jnp.int32, (size, size), 0)
        < lax.broadcasted_iota(jnp.int32, (size, size), 1),
        1.0,
        0.0,
    )
    before = nn(hot.astype(BF16), earlier.astype(BF16))
    rank = jnp.sum(hot * before, axis=0, keepdims=True).astype(jnp.int32)
    kept = live & (rank < CAP)
    target = jnp.where(kept, route_row[...] * CAP + rank, -1)
    match = lax.broadcasted_iota(jnp.int32, (experts * CAP, size), 0) == target
    match = jnp.where(match, 1.0, 0.0).astype(BF16)
    return mixed, inv, unit, hidden, probs, hot_col, gate, match


def expert_kernel(
    n_exp, n_col, n_row, experts,
    length, tok, attn, vectors, route_row, cot, w_in, w_out,
    out, rows, grads, acted, grad_before,
    sent, arrived, part, held, total, sums, s_a, r_a, s_b, r_b, s_c, r_c, s_d, r_d,
):
    n = n_exp * n_col
    r = lax.axis_index("row")
    me = lax.axis_index("exp") * n_col + lax.axis_index("col")
    peers = ring("row", n_row)
    group = group_peers(n_exp, n_col)
    ids = [{"exp": p // n_col, "col": lax.rem(p, n_col)} for p in group]
    everyone = [{"row": p} for p in peers] + ids
    greet(everyone)
    _, _, _, hidden, _, _, gate, match = middle(
        length[0], tok, attn, vectors, experts, route_row
    )
    grad = (gate * cot[...].astype(F32)).astype(BF16)
    first = nn(match, hidden).reshape(n, CAP, -1)
    second = nn(match, grad).reshape(n, CAP, -1)
    sent[...] = jnp.concatenate([first, second], axis=1).astype(BF16)
    meet(everyone)
    copies = [
        remote(sent.at[p], arrived.at[me], s_a.at[k], r_a.at[k], ids[k]) for k, p in enumerate(group)
    ]
    arrived[me] = sent[me]
    for copy in copies:
        copy.wait()
    both = arrived[...].astype(F32)
    rows[...] = both[:, :CAP].reshape(n * CAP, -1).astype(BF16)
    grads[...] = both[:, CAP:].reshape(n * CAP, -1).astype(BF16)
    before = nn(rows[...], w_in[0])
    scale = np.float32(np.sqrt(2 / np.pi))
    inner = jnp.tanh(scale * (before + 0.044715 * before * before * before))
    acted[...] = (0.5 * before * (1.0 + inner)).astype(BF16)
    slope = 0.5 * (1.0 + inner) + 0.5 * before * (1.0 - inner * inner) * scale * (
        1.0 + 3 * 0.044715 * before * before
    )
    result = nn(acted[...], w_out[0])
    grad_before[...] = (slope * nt(grads[...], w_out[0])).astype(BF16)
    back = nt(grad_before[...], w_in[0])
    both = jnp.concatenate([result.reshape(n, CAP, -1), back.reshape(n, CAP, -1)], axis=1)
    wide = both.shape[2] // n_row
    for b in range(n_row):
        part[b] = both[:, :, b * wide : (b + 1) * wide].astype(BF16)
    copies = [
        remote(part.at[p], held.at[k], s_b.at[k], r_b.at[k], {"row": p}) for k, p in enumerate(peers)
    ]
    acc = part[r].astype(F32)
    for k, copy in enumerate(copies):
        copy.wait_recv()
        acc = acc + held[k].astype(F32)
    total[...] = acc.astype(BF16)
    copies += [
        remote(total.at[p], sums.at[me], s_c.at[k], r_c.at[k], ids[k]) for k, p in enumerate(group)
    ]
    sums[me] = total[me]
    for copy in copies[n_row - 1 :]:
        copy.wait_recv()
    out[r] = sums[...]
    last = [
        remote(sums, out.at[r], s_d.at[k], r_d.at[k], {"row": p}) for k, p in enumerate(peers)
    ]
    for copy in copies:
        copy.wait_send()
    for copy in last:
        copy.wait()


def output_kernel(
    experts, rows, grads, acted, grad_before, result_in, gt_in, gwo, smo,
    result, gt, g_qkv, g_out, g_table, g_one, g_two, g_router, grad_in, grad_out,
):
    grad_in[0] = tn(rows[...], grad_before[...])
    grad_out[0] = tn(acted[...], grads[...])
    result[...] = result_in[...]
    for b in range(gt_in.shape[0]):
        block = gt_in.shape[1]
        gt[b * block : (b + 1) * block] = gt_in[b]
    g_qkv[...] = gwo[0:3]
    g_out[...] = gwo[3].T
    shard = gwo.shape[1]
    lines = experts + 2
    g_table[...] = smo[lines : lines + g_table.shape[1], : g_table.shape[0]].T
    g_one[...] = smo[experts + 1 : experts + 2, :shard]
    g_two[...] = smo[experts : experts + 1, :shard]
    g_router[...] = smo[0:experts, :shard]


def backward_kernel(
    n_exp, n_col, n_row, experts,
    length, tok, attn, vectors, route_row, cot, back_parts, hid, qkv, heads, w, rel, picks,
    result, gt, gwo, smo,
    gproj, gw, gm, gh, sm, hrow, sib, pre, zheld, smheld, smrow, go, sib_o, pre_o, zheld_o,
    s_row, r_row, s_row2, r_row2, s_sib, r_sib, s_z, r_z, s_sm, r_sm, s_sm2, r_sm2, s_so, r_so, s_zo, r_zo,
):
    e = lax.axis_index("exp")
    c = lax.axis_index("col")
    r = lax.axis_index("row")
    n = n_exp * n_col
    me = e * n_col + c
    rows = ring("row", n_row)
    exps = ring("exp", n_exp)
    group = group_peers(n_exp, n_col)
    ids = [{"exp": p // n_col, "col": lax.rem(p, n_col)} for p in group]
    everyone = [{"row": p} for p in rows] + ids
    greet(everyone)
    size, width = tok.shape
    block = size // n_row
    shard = width // n
    local = qkv.shape[2]

    def place(m, grad):
        for k in range(n):
            piece = grad[k * shard : (k + 1) * shard].astype(BF16)
            if m == 3:
                go[k % n_col, k // n_col] = piece
            else:
                gw[k % n_col, k // n_col, m] = piece

    mixed, inv, unit, hidden, probs, hot_col, gate, match = middle(
        length[0], tok, attn, vectors, experts, route_row
    )
    both = jnp.concatenate([back_parts[b].astype(F32) for b in range(n_row)], axis=-1)
    router = vectors[0:experts].astype(BF16)
    gain_one = vectors[experts : experts + 1]
    gain_two = vectors[experts + 1 : experts + 2]
    out_rows = both[:, :CAP].reshape(n * CAP, -1).astype(BF16)
    back_rows = both[:, CAP:].reshape(n * CAP, -1).astype(BF16)
    expert_result = tn(match, out_rows)
    upstream = cot[...].astype(F32)
    result[...] = (mixed + gate * expert_result).astype(BF16)
    grad_gate = jnp.sum(upstream * expert_result, axis=-1, keepdims=True)
    grad_logits = probs * (hot_col * grad_gate - gate * grad_gate)
    grad_low = grad_logits.astype(BF16)
    grad_rest = (grad_logits - grad_low.astype(F32)).astype(BF16)
    grad_router = tn(grad_low, hidden) + tn(grad_rest, hidden)
    grad_hidden = tn(match, back_rows) + nn(grad_low, router) + nn(grad_rest, router)
    grad_gain_two = jnp.sum(grad_hidden * unit, axis=0, keepdims=True)
    scaled = grad_hidden * gain_two
    gm[...] = upstream + inv * (scaled - unit * jnp.mean(scaled * unit, axis=-1, keepdims=True))
    gattn = gm[...].astype(BF16)
    place(3, tn(gattn, heads[...]))
    meet(everyone)
    sibling_o = remote(go.at[1 - c], sib_o, s_so, r_so, {"col": 1 - c})
    grad_heads = nn(gattn, w[3]).astype(BF16)
    flip = jnp.where(
        lax.broadcasted_iota(jnp.int32, (size, size), 0)
        + lax.broadcasted_iota(jnp.int32, (size, size), 1)
        == size - 1,
        1.0,
        0.0,
    ).astype(BF16)
    sm[...] = jnp.zeros(sm.shape, F32)
    lines = experts + 2
    for h in range(local // DH):
        at = slice(h * DH, (h + 1) * DH)
        q, k, v = qkv[0, :, at], qkv[1, :, at], qkv[2, :, at]
        probs_full = head_probs(q, k, bias_grid(rel[h : h + 1], size), length[0])
        gheads = grad_heads[:, at]
        gprobs = nt(gheads, v)
        dot = jnp.sum(probs_full * gprobs, axis=-1, keepdims=True)
        gscores = (probs_full * (gprobs - dot)).astype(BF16)
        gproj[2, :, at] = tn(probs_full.astype(BF16), gheads).astype(BF16)
        gproj[0, :, at] = (nn(gscores, k) * DH ** (-0.5)).astype(BF16)
        gproj[1, :, at] = (tn(gscores, q) * DH ** (-0.5)).astype(BF16)
        turned = nn(flip, gscores)
        turned = jnp.concatenate([turned, jnp.zeros((size, size), F32)], axis=1)
        turned = pltpu.roll(turned, 0, 1, stride=1, stride_axis=0)
        diagonal = jnp.sum(turned, axis=0, keepdims=True)
        line = nt(diagonal, picks[...].astype(F32), highest)
        for k in range(n):
            sm[k, lines + h : lines + h + 1, 0 : line.shape[1]] = line
    sibling_o.wait_recv()
    pre_o[...] = (go[c].astype(F32) + sib_o[...].astype(F32)).astype(BF16)
    z_copies_o = [
        remote(pre_o.at[p], zheld_o.at[k], s_zo.at[k], r_zo.at[k], {"exp": p})
        for k, p in enumerate(exps)
    ]
    row_copies = []
    grad_gain_one = jnp.zeros((1, width), F32)
    for k, p in enumerate(rows + [r]):
        at = pl.ds(pl.multiple_of(p * block, block), block)
        ghid = nt(gproj[0, at, :], w[0]) + nt(gproj[1, at, :], w[1]) + nt(gproj[2, at, :], w[2])
        rows_in = tok[at, :].astype(F32)
        inv_one = lax.rsqrt(jnp.mean(rows_in * rows_in, axis=-1, keepdims=True) + epsilon)
        unit_one = rows_in * inv_one
        grad_gain_one = grad_gain_one + jnp.sum(ghid * unit_one, axis=0, keepdims=True)
        if k < n_row - 1:
            gh[k] = ghid.astype(BF16)
            row_copies.append(remote(gh.at[k], hrow.at[k], s_row.at[k], r_row.at[k], {"row": p}))
    for m in range(3):
        place(m, tn(hid[...], gproj[m]))
    sibling = remote(gw.at[1 - c], sib, s_sib, r_sib, {"col": 1 - c})
    for k in range(n):
        at = slice(k * shard, (k + 1) * shard)
        sm[k, 0:experts, 0:shard] = grad_router[:, at]
        sm[k, experts : experts + 1, 0:shard] = grad_gain_two[:, at]
        sm[k, experts + 1 : experts + 2, 0:shard] = grad_gain_one[:, at]
    small = [
        remote(sm.at[p], smheld.at[k], s_sm.at[k], r_sm.at[k], ids[k]) for k, p in enumerate(group)
    ]
    sibling.wait_recv()
    pre[...] = (gw[c].astype(F32) + sib[...].astype(F32)).astype(BF16)
    z_copies = [
        remote(pre.at[p], zheld.at[k], s_z.at[k], r_z.at[k], {"exp": p}) for k, p in enumerate(exps)
    ]
    total = ghid
    for k, copy in enumerate(row_copies):
        copy.wait_recv()
        total = total + hrow[k].astype(F32)
    scaled = total * gain_one
    own = pl.ds(pl.multiple_of(r * block, block), block)
    gt[r] = (
        gm[own, :]
        + inv_one * (scaled - unit_one * jnp.mean(scaled * unit_one, axis=-1, keepdims=True))
    ).astype(BF16)
    row_copies2 = [
        remote(gt.at[r], gt.at[r], s_row2.at[k], r_row2.at[k], {"row": p}) for k, p in enumerate(rows)
    ]
    part = sm[me]
    for k, copy in enumerate(small):
        copy.wait_recv()
        part = part + smheld[k]
    smrow[0] = part
    small2 = [
        remote(smrow.at[0], smrow.at[k + 1], s_sm2.at[k], r_sm2.at[k], {"row": p})
        for k, p in enumerate(rows)
    ]
    full = part
    for k, copy in enumerate(small2):
        copy.wait_recv()
        full = full + smrow[k + 1]
    row_at = lax.broadcasted_iota(jnp.int32, part.shape, 0)
    smo[...] = jnp.where(row_at == experts + 1, full, part)
    wsum = pre[e].astype(F32)
    for k, copy in enumerate(z_copies):
        copy.wait_recv()
        wsum = wsum + zheld[k].astype(F32)
    gwo[0:3] = wsum
    osum = pre_o[e].astype(F32)
    for k, copy in enumerate(z_copies_o):
        copy.wait_recv()
        osum = osum + zheld_o[k].astype(F32)
    gwo[3] = osum
    for copy in [sibling, sibling_o] + z_copies_o + row_copies + small + z_copies + small2:
        copy.wait_send()
    for copy in row_copies2:
        copy.wait()


def bucket_picks(length, buckets):
    offset = np.arange(2 * length) - (length - 1)
    distance = np.abs(offset)
    beyond = np.sum(distance[:, None] >= thresholds, axis=-1)
    bucket = (offset > 0) * 16 + np.minimum(distance, 8) + beyond
    return (bucket[:, None] == np.arange(buckets)[None, :]).astype(np.float32)


def body(
    n_exp, n_col, n_row,
    tokens, qkv_weight, out_weight, bias_table, gain_attn, gain_expert, router_weight,
    expert_in, expert_out, lengths, routes, cotangent,
):
    n = n_exp * n_col
    size, width = tokens.shape
    shard = width // n
    local = qkv_weight.shape[2]
    heads_local = local // DH
    experts = router_weight.shape[1]
    lines = -(-(experts + 2) // 16) * 16
    dma = lambda k: pltpu.SemaphoreType.DMA((k,))
    picks = jnp.asarray(bucket_picks(size, bias_table.shape[0]).T, BF16)
    route_row = routes.reshape(1, size)
    block = size // n_row
    w, hid, qkv, heads, attn, vectors, rel = call(
        functools.partial(forward_kernel, n_exp, n_col, n_row),
        [
            ((4, width, local), BF16),
            ((size, width), BF16),
            ((3, size, local), BF16),
            ((size, local), BF16),
            ((n_row, block, width), BF16),
            ((lines, width), F32),
            ((heads_local, 2 * size), F32),
        ],
        [
            lengths, tokens, qkv_weight, out_weight, gain_attn.reshape(1, shard),
            gain_expert.reshape(1, shard), router_weight, bias_table, picks,
        ],
        [
            pltpu.VMEM((heads_local, size, size), F32),
            pltpu.VMEM((n_row, block, width), BF16),
            pltpu.VMEM((n_row - 1, block, width), BF16),
            pltpu.VMEM((lines, 128), F32),
            pltpu.VMEM((n_exp, n_col, lines, 128), F32),
            pltpu.VMEM((n_exp, n_col, 3, shard, local), BF16),
            pltpu.VMEM((shard, local), BF16),
            pltpu.VMEM((n_exp, n_col, shard, local), BF16),
        ]
        + [dma(n_row - 1)] * 4
        + [dma(n_exp - 1)] * 6
        + [dma(n_exp)] * 6,
        2,
        specs=[SMEM] + [VMEM] * 8,
    )
    attn = attn.reshape(size, width)
    slots = pltpu.VMEM((n, 2 * CAP, width), BF16)
    wide = width // n_row
    back, *saved = call(
        functools.partial(expert_kernel, n_exp, n_col, n_row, experts),
        [
            ((n_row, n, 2 * CAP, wide), BF16),
            ((n * CAP, width), BF16),
            ((n * CAP, width), BF16),
            ((n * CAP, expert_in.shape[2]), BF16),
            ((n * CAP, expert_in.shape[2]), BF16),
        ],
        [lengths, tokens, attn, vectors, route_row, cotangent, expert_in, expert_out],
        [
            slots, slots,
            pltpu.VMEM((n_row, n, 2 * CAP, wide), BF16),
            pltpu.VMEM((n_row - 1, n, 2 * CAP, wide), BF16),
            pltpu.VMEM((n, 2 * CAP, wide), BF16),
            pltpu.VMEM((n, 2 * CAP, wide), BF16),
            dma(n - 1), dma(n - 1), dma(n_row - 1), dma(n_row - 1),
            dma(n - 1), dma(n - 1), dma(n_row - 1), dma(n_row - 1),
        ],
        3,
        specs=[SMEM] + [VMEM] * 7,
    )
    high = -(-(experts + 2 + heads_local) // 8) * 8
    result, gt, gwo, smo = call(
        functools.partial(backward_kernel, n_exp, n_col, n_row, experts),
        [
            ((size, width), BF16),
            ((n_row, block, width), BF16),
            ((4, shard, local), F32),
            ((high, 128), F32),
        ],
        [
            lengths, tokens, attn, vectors, route_row, cotangent, back, hid, qkv, heads, w, rel,
            picks,
        ],
        [
            pltpu.VMEM((3, size, local), BF16),
            pltpu.VMEM((n_col, n_exp, 3, shard, local), BF16),
            pltpu.VMEM((size, width), F32),
            pltpu.VMEM((n_row - 1, block, width), BF16),
            pltpu.VMEM((n, high, 128), F32),
            pltpu.VMEM((n_row - 1, block, width), BF16),
            pltpu.VMEM((n_exp, 3, shard, local), BF16),
            pltpu.VMEM((n_exp, 3, shard, local), BF16),
            pltpu.VMEM((n_exp - 1, 3, shard, local), BF16),
            pltpu.VMEM((n - 1, high, 128), F32),
            pltpu.VMEM((n_row, high, 128), F32),
            pltpu.VMEM((n_col, n_exp, shard, local), BF16),
            pltpu.VMEM((n_exp, shard, local), BF16),
            pltpu.VMEM((n_exp, shard, local), BF16),
            pltpu.VMEM((n_exp - 1, shard, local), BF16),
            dma(n_row - 1), dma(n_row - 1), dma(n_row - 1), dma(n_row - 1),
            pltpu.SemaphoreType.DMA, pltpu.SemaphoreType.DMA,
            dma(n_exp - 1), dma(n_exp - 1),
            dma(n - 1), dma(n - 1), dma(n_row - 1), dma(n_row - 1),
            pltpu.SemaphoreType.DMA, pltpu.SemaphoreType.DMA,
            dma(n_exp - 1), dma(n_exp - 1),
        ],
        4,
        specs=[SMEM] + [VMEM] * 12,
    )
    (
        result, gt, g_qkv, g_out, g_table, g_one, g_two, g_router, grad_in, grad_out,
    ) = call(
        functools.partial(output_kernel, experts),
        [
            ((size, width), BF16),
            ((size, width), BF16),
            (qkv_weight.shape, F32),
            (out_weight.shape, F32),
            (bias_table.shape, F32),
            ((1, shard), F32),
            ((1, shard), F32),
            ((experts, shard), F32),
            (expert_in.shape, F32),
            (expert_out.shape, F32),
        ],
        [*saved, result, gt, gwo, smo],
    )
    return (
        result, gt, g_qkv, g_out, g_table, g_one.reshape(shard), g_two.reshape(shard), g_router.T,
        grad_in, grad_out,
    )


def solution(mesh):
    both = ("exp", "col")
    placed = (
        P(both, None),
        P(None, both, "row"),
        P("row", both),
        P(None, "row"),
        P(both),
        P(both),
        P(both, None),
        P(both, None, "row"),
        P(both, "row", None),
        P(both),
        P(both, None),
        P(both, None),
    )
    shape = mesh.shape
    return jax.shard_map(
        functools.partial(body, shape["exp"], shape["col"], shape["row"]),
        mesh=mesh,
        in_specs=placed,
        out_specs=(
            P(both, None),
            P(both, None),
            P(None, both, "row"),
            P("row", both),
            P(None, "row"),
            P(both),
            P(both),
            P(both, None),
            P(both, None, "row"),
            P(both, "row", None),
        ),
        check_vma=False,
    )
```

time: 148 us -> 127 us (0.86)
  local copies, waits for them, and re-layouts: 15.3 us -> 4.12 us
  Pallas kernels: 126 us -> 121 us
  other arithmetic: 2.95 us -> 0 us
  matrix products: 1.57 us -> 0 us
    pallas_call x5 -> x4, Pallas kernels: 126 us -> 121 us  [call(): pl.pallas_call(kernel, out_shape=[jax.ShapeDtypeStruct(s, d) for s, d in...]
    transpose x3 -> x0, local copies, waits for them, and re-layouts: 3.43 us -> none  [the longest x1 1.27 us: body(): smo[:experts, :shard]]
    concatenate x2 -> x0, other arithmetic: 2.94 us -> none  [the longest x1 1.63 us: body(): packed = jnp.concatenate([qkv_weight, out_weight.T[None]], axis=0)]
    unnamed x10 -> x3, local copies, waits for them, and re-layouts: 6.88 us -> 4.12 us
    slice x3 -> x0, local copies, waits for them, and re-layouts: 2.39 us -> none  [the longest x1 1.69 us: body(): gwo[:3]]
    dot_general x1 -> x0, matrix products: 1.57 us -> none  [body(): jnp.dot(bias_table.T, jnp.asarray(picks.T, BF16), preferred_element_type=...]
where the time goes in v3:
time: 127 us
  Pallas kernels  121 us (95%)
  local copies, waits for them, and re-layouts  4.12 us (3%)
  between operations  1.32 us (1%)
    pallas_call x4, Pallas kernels, call(): pl.pallas_call(kernel, out_shape=[jax.ShapeDtypeStruct(s, d) for s, d in...  121 us
    unnamed x3, local copies, waits for them, and re-layouts  4.12 us

profile of v3, /device:TPU:0, one launch (start us, length us, event | category | flops | bytes accessed | tf_op | source)
XLA Modules:
  0.0 126.5 jit_solution(14550471527412698578)
XLA Ops:
  1.3 1.4 %copy.24.table = bf16[32,3]{1,0:T(8,128)(2,1)} copy(bf16[32,3]{0,1:T(4,128)(2,1)} %param.16) | data formatting | bytes 384 | tf_op args[3]
  2.7 1.4 %copy.23.router = bf16[96,8]{1,0:T(8,128)(2,1)} copy(bf16[96,8]{0,1:T(8,128)(2,1)} %param.19) | data formatting | bytes 3072 | tf_op args[6]
  4.0 50.0 %shard_map.204 = (bf16[4,768,192]{2,1,0:T(8,128)(2,1)}, bf16[512,768]{1,0:T(8,128)(2,1)}, bf16[3,512,192]{2,1,0:T(8,128)(2,1)}, bf16[512,192]{1,0:T(8,128)(2,1)}...) custom-call(s32[1]{0:T(128)S(6)} %copy.26.length, bf16[512,768]{1,0:T(8,128)(2,1)} %tok.5, ...), custom_call_target="tpu_custom_call" | custom-call | tf_op jit(solution)/shard_map/pallas_call | solution.py:44
  54.1 30.8 %shard_map.205 = (bf16[4,8,16,192]{3,2,1,0:T(8,128)(2,1)}, bf16[64,768]{1,0:T(8,128)(2,1)}, bf16[64,768]{1,0:T(8,128)(2,1)}, bf16[64,768]{1,0:T(8,128)(2,1)}, bf16[64,768]{1,0:T(8,128)(2,1)}) custom-call(s32[1]{0:T(128)S(6)} %copy.26.length, bf16[512,768]{1,0:T(8,128)(2,1)} %tok.5, bf16[512,768]{1,0:T(8,128)(2,1)} %bitcast.7, ...), custom_call_target="tpu_custom_call" | custom-call | tf_op jit(solution)/shard_map/pallas_call | solution.py:44
  84.8 35.0 %shard_map.206 = (bf16[512,768]{1,0:T(8,128)(2,1)}, bf16[4,128,768]{2,1,0:T(8,128)(2,1)}, f32[4,96,192]{2,1,0:T(8,128)}, f32[16,128]{1,0:T(8,128)}) custom-call(s32[1]{0:T(128)S(6)} %copy.26.length, bf16[512,768]{1,0:T(8,128)(2,1)} %tok.5, bf16[512,768]{1,0:T(8,128)(2,1)} %bitcast.8, f32[16,768]{1,0:T(8,128)} %get-tuple-element.37.vectors, ...), custom_call_target="tpu_custom_call" | custom-call | tf_op jit(solution)/shard_map/pallas_call | solution.py:44
  119.9 5.2 %shard_map.207 = (bf16[512,768]{1,0:T(8,128)(2,1)}, bf16[512,768]{1,0:T(8,128)(2,1)}, f32[3,96,192]{2,1,0:T(8,128)}, f32[192,96]{1,0:T(8,128)}, f32[32,3]{1,0:T(...) custom-call(bf16[64,768]{1,0:T(8,128)(2,1)} %get-tuple-element.38.ro, ...), custom_call_target="tpu_custom_call" | custom-call | tf_op jit(solution)/shard_map/pallas_call | solution.py:44
  125.1 1.4 %copy.25 = f32[32,3]{0,1:T(4,128)} copy(f32[32,3]{1,0:T(8,128)} %get-tuple-element.66) | data formatting | bytes 768
